TPU v7x, 256 devices: a whole 4x4x8 slice. The times are simulated.
256 devices in a mesh: blk: 256 (over y, x, z, core).
Axes of the slice: x: 4, y: 4, z: 8, core: 2. Of those that a mesh axis runs over, the one named last changes fastest.
Arguments:
- integrals: float32 [131072, 2176], P('blk'), may hold values from -0.125 to 0.125
- tile_pattern: int32 [1024, 17], P('blk'), may hold values 0 or 1
- amplitudes: float32 [131072, 1280], P('blk'), may hold values from -6 to 6
- residual_in: float32 [131072, 1280], P('blk'), may hold values from -6 to 6
Outputs:
- residual: float32 [131072, 1280], P('blk')
Inputs may be any that keep to these rules, and one draw needn't show every extreme that they name: `tile_pattern`: 1 where the integral tile is significant, 0 where it is neglected.
All inputs are finite; a program needn't handle non-finite values. No bound on the sum of `tile_pattern` on one device may be relied on, other than what follows from the above.
Results may differ from a plain program's by a relative error of at most 0.0003.
Values sent between devices are 32-bit elements; how exact they have to be, the bound alone decides.
No kernel may reach another device: no remote copies, remote signals or barrier semaphores. Data moves between devices by JAX's collectives and lax.ppermute only.
A program may use at most 64 MiB of HBM per device.

v0:
```python
import jax
import jax.numpy as jnp
from jax import lax
from jax.sharding import PartitionSpec as P

TB = 128
W = 8


def passed_along(value, axis, steps):
    count = lax.axis_size(axis)
    pairs = [(source, (source + steps) % count) for source in range(count)]
    return lax.ppermute(value, axis, pairs)


def per_device(integrals, tile_pattern, amplitudes, residual_in):
    band = 2 * W + 1
    tiles_here = integrals.shape[0] // TB
    steps_out = W // tiles_here
    mask = jnp.repeat(tile_pattern.astype(jnp.float32), TB, axis=1)
    masked = integrals.reshape(tiles_here, TB, band * TB) * mask[:, None, :]
    lowers = []
    uppers = []
    below = amplitudes
    above = amplitudes
    for step in range(steps_out):
        below = passed_along(below, "blk", 1)
        above = passed_along(above, "blk", -1)
        lowers.append(below)
        uppers.append(above)
    pieces = list(reversed(lowers)) + [amplitudes] + uppers
    window = jnp.concatenate(pieces, 0)
    blocks = []
    for row_tile in range(tiles_here):
        rows = window[row_tile * TB : (row_tile + band) * TB]
        blocks.append(
            jnp.dot(
                masked[row_tile],
                rows,
                precision=lax.Precision.HIGHEST,
                preferred_element_type=jnp.float32,
            )
        )
    ladder = jnp.concatenate(blocks, 0)
    return residual_in + ladder


def solution(mesh):
    return jax.shard_map(
        per_device,
        mesh=mesh,
        in_specs=(P("blk", None), P("blk", None), P("blk", None), P("blk", None)),
        out_specs=P("blk", None),
        check_vma=False,
    )
```

profile of v0, /device:TPU:0, one launch (start us, length us, event | category | flops | bytes accessed | tf_op | source)
XLA Modules:
  0.0 101.2 jit_solution(16803882466457454323)
XLA Ops:
  0.0 0.0 collective-permute-start
  0.0 8.2 %collective-permute-start.2 = (f32[512,1280]{1,0:T(8,128)}, f32[512,1280]{1,0:T(8,128)S(1)}, u32[]{:S(2)}, u32[]{:S(2)}) collective-permute-start(f32[512,1280]{1,0:T(8,128)} %param.6), channel_id=1, source_target_pairs={{0,255},{1,0},{2,1},{3,2},{4,3},{5,4},{6,5},{7,6},{8,7},{9,8},{10,... | collective-permute-start | bytes 7864328 | tf_op jit(solution)/shard_map/ppermute | solution.py:13
  8.2 29.5 %collective-permute-done = f32[512,1280]{1,0:T(8,128)S(1)} collective-permute-done((f32[512,1280]{1,0:T(8,128)}, f32[512,1280]{1,0:T(8,128)S(1)}, u32[]{:S(2)}, u32[]{:S(2)}) %collective-permute-start) | collective-permute-done | bytes 2621472 | tf_op jit(solution)/shard_map/ppermute | solution.py:13
  37.8 0.0 collective-permute-start.1
  37.8 0.0 collective-permute-done.2
  37.8 7.2 %collective-permute-start.3 = (f32[512,1280]{1,0:T(8,128)S(1)}, f32[512,1280]{1,0:T(8,128)S(1)}, u32[]{:S(2)}, u32[]{:S(2)}) collective-permute-start(f32[512,1280]{1,0:T(8,128)S(1)} %collective-permute-done.2), channel_id=1, source_target_pairs={{0,255},{1,0},{2,1},{3,2},{4,3},{5,4},{6,5},{7,6},{8,7},{9,8},{10,... | collective-permute-start | bytes 7864328 | tf_op jit(solution)/shard_map/ppermute | solution.py:13
  44.9 0.7 convert_element_type.3
  45.6 0.1 broadcast_bitcast_fusion
  45.7 2.6 %broadcast_multiply_fusion = f32[4,128,2176]{2,1,0:T(8,128)S(1)} fusion(f32[4,128,2176]{2,1,0:T(8,128)} %bitcast.18, f32[4,2176]{1,0:T(4,128)S(1)} %bitcast.19), kind=kLoop, calls=%fused_computation.9 | loop fusion | flops 1114112 | bytes 8947712 | tf_op jit(solution)/shard_map/mul | solution.py:21
  48.3 0.0 copy-start
  48.3 25.9 %collective-permute-done.1 = f32[512,1280]{1,0:T(8,128)S(1)} collective-permute-done((f32[512,1280]{1,0:T(8,128)S(1)}, f32[512,1280]{1,0:T(8,128)S(1)}, u32[]{:S(2)}, u32[]{:S(2)}) %collective-permute-start.1) | collective-permute-done | bytes 2621472 | tf_op jit(solution)/shard_map/ppermute | solution.py:13
  74.3 0.2 constant_dynamic-update-slice_fusion.4
  74.4 0.2 constant_dynamic-update-slice_fusion.3
  74.6 0.0 copy-done
  74.6 0.2 constant_dynamic-update-slice_fusion.2
  74.8 0.2 constant_dynamic-update-slice_fusion.1
  75.0 0.0 collective-permute-done.3
  75.0 0.2 constant_dynamic-update-slice_fusion
  75.2 6.0 %fusion = f32[128,1280]{1,0:T(8,128)S(1)} fusion(f32[2560,1280]{1,0:T(8,128)S(1)} %constant_dynamic-update-slice_fusion, f32[4,128,2176]{2,1,0:T(8,128)S(1)} %broadcast_multiply_fusion), kind=kOutput, calls=%fused_computation | convolution fusion | flops 4278190080 | bytes 12910592 | tf_op jit(solution)/shard_map/dot_general | solution.py:37
  81.2 6.2 %fusion.2 = f32[128,1280]{1,0:T(8,128)S(1)} fusion(f32[2560,1280]{1,0:T(8,128)S(1)} %constant_dynamic-update-slice_fusion, f32[4,128,2176]{2,1,0:T(8,128)S(1)} %broadcast_multiply_fusion), kind=kOutput, calls=%fused_computation.2 | convolution fusion | flops 4278190080 | bytes 12910592 | tf_op jit(solution)/shard_map/dot_general | solution.py:37
  87.4 6.0 %fusion.4 = f32[128,1280]{1,0:T(8,128)S(1)} fusion(f32[2560,1280]{1,0:T(8,128)S(1)} %constant_dynamic-update-slice_fusion, f32[4,128,2176]{2,1,0:T(8,128)S(1)} %broadcast_multiply_fusion), kind=kOutput, calls=%fused_computation.4 | convolution fusion | flops 4278190080 | bytes 12910592 | tf_op jit(solution)/shard_map/dot_general | solution.py:37
  93.4 0.0 copy-start.1
  93.4 6.0 %fusion.6 = f32[128,1280]{1,0:T(8,128)S(1)} fusion(f32[2560,1280]{1,0:T(8,128)S(1)} %constant_dynamic-update-slice_fusion, f32[4,128,2176]{2,1,0:T(8,128)S(1)} %broadcast_multiply_fusion), kind=kOutput, calls=%fused_computation.6 | convolution fusion | flops 4278190080 | bytes 12910592 | tf_op jit(solution)/shard_map/dot_general | solution.py:37
  99.4 0.0 copy-done.1
  99.4 1.8 %maximum_add_fusion = f32[512,1280]{1,0:T(8,128)} fusion(f32[512,1280]{1,0:T(8,128)S(1)} %copy-done.1, f32[128,1280]{1,0:T(8,128)S(1)} %fusion, f32[128,1280]{1,0:T(8,128)S(1)} %fusion.2, f32[128,1280]{1,0:T(8,128)S(1)} %fusion.4, f32[128,1280]{1,0:T(8,128)S(1)} %fusion.6), kind=kLoop, calls=%fused_computation.8 | loop fusion | flops 2621440 | bytes 7864320 | tf_op jit(solution)/shard_map/add | solution.py:45
  (1 shorter events, 0.0 us)
Async XLA Ops:
  0.0 37.8 %collective-permute-start = (f32[512,1280]{1,0:T(8,128)}, f32[512,1280]{1,0:T(8,128)S(1)}, u32[]{:S(2)}, u32[]{:S(2)}) collective-permute-start(f32[512,1280]{1,0:T(8,128)} %param.6), channel_id=1, source_target_pairs={{0,1},{1,2},{2,3},{3,4},{4,5},{5,6},{6,7},{7,8},{8,9},{9,10},{10,1... | collective-permute-start | bytes 7864328 | tf_op jit(solution)/shard_map/ppermute | solution.py:13
  0.0 37.8 %collective-permute-start.2 = (f32[512,1280]{1,0:T(8,128)}, f32[512,1280]{1,0:T(8,128)S(1)}, u32[]{:S(2)}, u32[]{:S(2)}) collective-permute-start(f32[512,1280]{1,0:T(8,128)} %param.6), channel_id=1, source_target_pairs={{0,255},{1,0},{2,1},{3,2},{4,3},{5,4},{6,5},{7,6},{8,7},{9,8},{10,... | collective-permute-start | bytes 7864328 | tf_op jit(solution)/shard_map/ppermute | solution.py:13
  37.8 36.5 %collective-permute-start.1 = (f32[512,1280]{1,0:T(8,128)S(1)}, f32[512,1280]{1,0:T(8,128)S(1)}, u32[]{:S(2)}, u32[]{:S(2)}) collective-permute-start(f32[512,1280]{1,0:T(8,128)S(1)} %collective-permute-done), channel_id=1, source_target_pairs={{0,1},{1,2},{2,3},{3,4},{4,5},{5,6},{6,7},{7,8},{8,9},{9,10},{10,1... | collective-permute-start | bytes 7864328 | tf_op jit(solution)/shard_map/ppermute | solution.py:13
  37.8 37.2 %collective-permute-start.3 = (f32[512,1280]{1,0:T(8,128)S(1)}, f32[512,1280]{1,0:T(8,128)S(1)}, u32[]{:S(2)}, u32[]{:S(2)}) collective-permute-start(f32[512,1280]{1,0:T(8,128)S(1)} %collective-permute-done.2), channel_id=1, source_target_pairs={{0,255},{1,0},{2,1},{3,2},{4,3},{5,4},{6,5},{7,6},{8,7},{9,8},{10,... | collective-permute-start | bytes 7864328 | tf_op jit(solution)/shard_map/ppermute | solution.py:13
  48.3 26.3 %copy-start = (f32[512,1280]{1,0:T(8,128)S(1)}, f32[512,1280]{1,0:T(8,128)}, u32[]{:S(2)}) copy-start(f32[512,1280]{1,0:T(8,128)} %param.6) | copy-start | bytes 7864324
  93.4 6.0 %copy-start.1 = (f32[512,1280]{1,0:T(8,128)S(1)}, f32[512,1280]{1,0:T(8,128)}, u32[]{:S(2)}) copy-start(f32[512,1280]{1,0:T(8,128)} %param.7) | copy-start | bytes 7864324
where the time goes:
time: 101 us
  waiting for transfers between devices  55.5 us (55%)
  matrix products  24.2 us (24%)
  starting transfers between devices  15.4 us (15%)
  other arithmetic  5.07 us (5%)
    ppermute x4, waiting for transfers between devices, passed_along(): return lax.ppermute(value, axis, pairs)  55.5 us
    dot_general x4, matrix products, per_device(): jnp.dot(masked[row_tile], rows, precision=lax.Precision.HIGHEST, preferre...  24.2 us
    ppermute x4, starting transfers between devices, passed_along(): return lax.ppermute(value, axis, pairs)  15.4 us
    mul x1, other arithmetic, per_device(): masked = integrals.reshape(tiles_here, TB, band * TB) * mask[:, None, :]  2.59 us
  transfers between devices with their start and end apart: 4, of which 2 were waited for; matrix products, arithmetic and copies ran while one was open for 4% of the time, Pallas kernels for 0%

commit v1 on v0

v1 whole, which is shorter than its diff:
```python
import functools

import jax
import jax.numpy as jnp
from jax import lax
from jax.experimental import pallas as pl
from jax.experimental.pallas import tpu as pltpu
from jax.sharding import PartitionSpec as P

TB = 128
W = 8
BAND = 2 * W + 1
AXIS = "blk"

OWN, PARTNER, FACING, BESIDE, BEYOND = range(5)


def exchange(value, offset):
    count = lax.axis_size(AXIS)
    pairs = []
    for low in range(offset, count + offset, 2):
        a, b = low % count, (low + 1) % count
        pairs += [(a, b), (b, a)]
    return lax.ppermute(value, AXIS, pairs)


def split(x):
    high = x.astype(jnp.bfloat16)
    low = (x - high.astype(jnp.float32)).astype(jnp.bfloat16)
    return high, low


def align_kernel(tiles, pattern_ref, v_ref, high_ref, low_ref):
    row = pl.program_id(0)
    odd = lax.rem(lax.axis_index(AXIS), 2)
    sign = 1 - 2 * odd
    for role, step in ((OWN, 0), (PARTNER, 1), (FACING, -1), (BESIDE, 2), (BEYOND, -2)):
        block = 2 + sign * step
        for t in range(tiles):
            k = block * tiles + t - row
            inside = jnp.logical_and(k >= 0, k < BAND)
            k = jnp.clip(k, 0, BAND - 1)
            keep = jnp.where(inside, pattern_ref[row, k], 0).astype(jnp.float32)
            tile = v_ref[:, pl.ds(pl.multiple_of(k * TB, TB), TB)] * keep
            high, low = split(tile)
            high_ref[role, :, t * TB : (t + 1) * TB] = high
            low_ref[role, :, t * TB : (t + 1) * TB] = low


def align(integrals, tile_pattern):
    rows = integrals.shape[0]
    tiles = rows // TB
    shape = jax.ShapeDtypeStruct((5, rows, rows), jnp.bfloat16)
    spec = pl.BlockSpec((5, TB, rows), lambda r: (0, r, 0))
    return pl.pallas_call(
        functools.partial(align_kernel, tiles),
        grid=(tiles,),
        in_specs=[
            pl.BlockSpec(memory_space=pltpu.SMEM),
            pl.BlockSpec((TB, BAND * TB), lambda r: (r, 0)),
        ],
        out_specs=[spec, spec],
        out_shape=[shape, shape],
        compiler_params=pltpu.CompilerParams(vmem_limit_bytes=24 * 2**20),
        cost_estimate=pl.CostEstimate(flops=10 * rows * rows, bytes_accessed=10**7, transcendentals=0),
        name="align",
    )(tile_pattern, integrals)


def add_kernel(count, *refs):
    *blocks, acc_ref, out_ref = refs
    total = acc_ref[...]
    for i in range(count):
        vh_ref, vl_ref, t_ref = blocks[3 * i : 3 * i + 3]
        th, tl = split(t_ref[...])
        vh, vl = vh_ref[0], vl_ref[0]
        dot = functools.partial(jnp.dot, preferred_element_type=jnp.float32)
        total += dot(vh, th) + (dot(vh, tl) + dot(vl, th))
    out_ref[...] = total


def add_products(acc, high, low, parts, cols, name):
    rows, width = acc.shape
    args, specs = [], []
    for role, piece, block in parts:
        deep = block.shape[0]
        spec = pl.BlockSpec((1, rows, deep), lambda j, role=role, piece=piece: (role, 0, piece))
        args += [high, low, block]
        specs += [spec, spec, pl.BlockSpec((deep, cols), lambda j: (0, j))]
    args.append(acc)
    specs.append(pl.BlockSpec((rows, cols), lambda j: (0, j)))
    n = len(parts)
    return pl.pallas_call(
        functools.partial(add_kernel, n),
        grid=(width // cols,),
        in_specs=specs,
        out_specs=pl.BlockSpec((rows, cols), lambda j: (0, j)),
        out_shape=jax.ShapeDtypeStruct(acc.shape, acc.dtype),
        compiler_params=pltpu.CompilerParams(vmem_limit_bytes=32 * 2**20),
        cost_estimate=pl.CostEstimate(flops=1, bytes_accessed=1, transcendentals=0),
        name=name,
    )(*args)


def last_kernel(start, step, *refs):
    high_ref, low_ref, block_ref, acc_ref = refs[:4]
    out_ref, stage, sems = refs[-3:]
    copies = []
    for i in range(block_ref.shape[1] // step):
        here = slice(i * step, i * step + step)
        there = slice(start + i * step, start + i * step + step)
        th, tl = split(block_ref[:, here])
        vh, vl = high_ref[BEYOND], low_ref[BEYOND]
        dot = functools.partial(jnp.dot, preferred_element_type=jnp.float32)
        stage[:, here] = acc_ref[:, there] + (dot(vh, th) + (dot(vh, tl) + dot(vl, th)))
        copies.append(pltpu.make_async_copy(stage.at[:, here], out_ref.at[:, there], sems.at[i]))
        copies[-1].start()
    for copy in copies:
        copy.wait()


def add_last(acc, high, low, block, start, out, name):
    rows, width = block.shape
    step = 256
    args = [high, low, block, acc]
    specs = [pl.BlockSpec(memory_space=pltpu.VMEM)] * 4
    aliases = {}
    if out is not None:
        aliases = {len(args): 0}
        args.append(out)
        specs.append(pl.BlockSpec(memory_space=pl.ANY))
    return pl.pallas_call(
        functools.partial(last_kernel, start, step),
        in_specs=specs,
        out_specs=pl.BlockSpec(memory_space=pl.ANY),
        out_shape=jax.ShapeDtypeStruct(acc.shape, acc.dtype),
        input_output_aliases=aliases,
        scratch_shapes=[pltpu.VMEM((rows, width), jnp.float32), pltpu.SemaphoreType.DMA((width // step,))],
        compiler_params=pltpu.CompilerParams(vmem_limit_bytes=16 * 2**20),
        cost_estimate=pl.CostEstimate(flops=1, bytes_accessed=1, transcendentals=0),
        name=name,
    )(*args)


def per_device(integrals, tile_pattern, amplitudes, residual_in):
    rows, width = amplitudes.shape
    facing = exchange(amplitudes, 1)
    high, low = align(integrals, tile_pattern)
    partner = exchange(amplitudes, 0)
    cuts = [0, 768, 1280]
    beyond = [exchange(partner[:, a:b], 1) for a, b in zip(cuts, cuts[1:])]
    acc = add_products(residual_in, high, low, [(OWN, 0, amplitudes), (PARTNER, 0, partner)], 256, "near")
    facing, acc = lax.optimization_barrier((facing, acc))
    n = rows // 4
    beside = [exchange(facing[i : i + n], 0) for i in range(0, rows, n)]
    parts = [(FACING, 0, facing)] + [(BESIDE, i, block) for i, block in enumerate(beside)]
    acc = add_products(acc, high, low, parts, 256, "middle")
    out = None
    for i, block in enumerate(beyond):
        out = add_last(acc, high, low, block, cuts[i], out, "last%d" % i)
    return out


def solution(mesh):
    return jax.shard_map(
        per_device,
        mesh=mesh,
        in_specs=(P("blk", None), P("blk", None), P("blk", None), P("blk", None)),
        out_specs=P("blk", None),
        check_vma=False,
    )
```

time: 101 us -> 68.7 us (0.68)
  waiting for transfers between devices: 55.5 us -> 26.5 us
  matrix products: 24.2 us -> 0 us
  Pallas kernels: 0 us -> 20.1 us
  other arithmetic: 5.07 us -> 0 us
  local copies, waits for them, and re-layouts: 0.96 us -> 4.93 us
  starting transfers between devices: 15.4 us -> 16.8 us
    ppermute x4 -> x8, waiting for transfers between devices: 55.5 us -> 26.5 us  [exchange(): return lax.ppermute(value, AXIS, pairs)]
    dot_general x4 -> x0, matrix products: 24.2 us -> none  [per_device(): jnp.dot(masked[row_tile], rows, precision=lax.Precision.HIGHEST, preferre...]
    pallas_call x0 -> x5, Pallas kernels: none -> 20.1 us  [the longest x2 13.6 us: add_products(): pl.pallas_call(functools.partial(add_kernel, n), grid=(width // cols,), i...]
    unnamed x10 -> x8, local copies, waits for them, and re-layouts: 0.78 us -> 4.45 us
    mul x1 -> x0, other arithmetic: 2.59 us -> none  [per_device(): masked = integrals.reshape(tiles_here, TB, band * TB) * mask[:, None, :]]
    add x1 -> x0, other arithmetic: 1.8 us -> none  [per_device(): return residual_in + ladder]
    ppermute x4 -> x8, starting transfers between devices: 15.4 us -> 16.8 us  [exchange(): return lax.ppermute(value, AXIS, pairs)]
  transfers between devices with their start and end apart: 4 -> 8, of which waited for: 2 -> 5; matrix products, arithmetic and copies ran while one was open for 4% -> 1% of each run, Pallas kernels for 0% -> 26%
where the time goes in v1:
time: 68.7 us; the launch traced here: 68.5 us
  waiting for transfers between devices  26.5 us (39%)
  Pallas kernels  20.1 us (29%)
  starting transfers between devices  16.8 us (24%)
  local copies, waits for them, and re-layouts  4.93 us (7%)
    ppermute x8, waiting for transfers between devices, exchange(): return lax.ppermute(value, AXIS, pairs)  26.5 us
    ppermute x8, starting transfers between devices, exchange(): return lax.ppermute(value, AXIS, pairs)  16.8 us
    pallas_call x2, Pallas kernels, add_products(): pl.pallas_call(functools.partial(add_kernel, n), grid=(width // cols,), i...  13.6 us
    unnamed x8, local copies, waits for them, and re-layouts  4.45 us
    pallas_call x2, Pallas kernels, add_last(): pl.pallas_call(functools.partial(last_kernel, start, step), in_specs=spec...  4.39 us
    pallas_call x1, Pallas kernels, align(): pl.pallas_call(functools.partial(align_kernel, tiles), grid=(tiles,), in_...  2.08 us
  transfers between devices with their start and end apart: 8, of which 5 were waited for; matrix products, arithmetic and copies ran while one was open for 1% of the time, Pallas kernels for 26%

profile of v1, /device:TPU:0, one launch (start us, length us, event | category | flops | bytes accessed | tf_op | source)
XLA Modules:
  0.0 68.5 jit_solution(1642045374474579803)
XLA Ops:
  0.0 0.0 collective-permute-start
  0.0 8.9 %collective-permute-start.2 = (f32[512,1280]{1,0:T(8,128)}, f32[512,1280]{1,0:T(8,128)S(1)}, u32[]{:S(2)}, u32[]{:S(2)}) collective-permute-start(f32[512,1280]{1,0:T(8,128)} %refs_2_.1), channel_id=1, source_target_pairs={{1,2},{2,1},{3,4},{4,3},{5,6},{6,5},{7,8},{8,7},{9,10},{10,9},{11,... | collective-permute-start | bytes 7864328 | tf_op jit(solution)/shard_map/ppermute | solution.py:24
  8.9 0.0 copy-start
  8.9 2.3 %copy-done = f32[512,2176]{1,0:T(8,128)S(1)} copy-done((f32[512,2176]{1,0:T(8,128)S(1)}, f32[512,2176]{1,0:T(8,128)}, u32[]{:S(2)}) %copy-start) | copy-done | bytes 4456472
  11.1 0.0 copy-start.3
  11.1 0.7 copy-done.3
  11.8 0.0 copy-start.2
  11.8 2.1 %align.1 = (bf16[5,512,512]{2,1,0:T(8,128)(2,1)S(1)}, bf16[5,512,512]{2,1,0:T(8,128)(2,1)S(1)}) custom-call(s32[4,17]{1,0:T(4,128)S(1)} %copy-done.3, f32[512,2176]{1,0:T(8,128)S(1)} %copy-done), custom_call_target="tpu_custom_call" | custom-call | flops 2621440 | bytes 10000000 | tf_op jit(solution)/shard_map/align/pallas_call | solution.py:55
  13.9 0.0 copy-start.1
  13.9 0.0 collective-permute-done.refs_5_
  13.9 0.1 slice.25
  14.1 0.1 collective-permute-start.7
  14.2 0.0 copy-done.2
  14.2 1.5 %copy-done.1 = f32[512,1280]{1,0:T(8,128)S(1)} copy-done((f32[512,1280]{1,0:T(8,128)S(1)}, f32[512,1280]{1,0:T(8,128)}, u32[]{:S(2)}) %copy-start.1) | copy-done | bytes 2621464
  15.7 5.6 %near.1.refs_15_ = f32[512,1280]{1,0:T(8,128)S(1)} custom-call(bf16[5,512,512]{2,1,0:T(8,128)(2,1)S(1)} %get-tuple-element.9.refs_0_.refs_3_.refs_6_.refs_9_.refs_12_, bf16[5,512,512]{2,1,0:T(8,128)(2,1)S(1)} %get-tuple-element.10.refs_1_.refs_4_.refs_7_.refs_10_.refs_13_, f32[512,1280]{1,0:T(8,128)S(1)} %copy-done.2, ...), custom_call_target="tpu_custom_call" | custom-call | flops 1 | bytes 1 | tf_op jit(solution)/shard_map/near/pallas_call | solution.py:93
  21.3 17.1 %collective-permute-done.2.refs_2_ = f32[512,1280]{1,0:T(8,128)S(1)} collective-permute-done((f32[512,1280]{1,0:T(8,128)}, f32[512,1280]{1,0:T(8,128)S(1)}, u32[]{:S(2)}, u32[]{:S(2)}) %collective-permute-start.2) | collective-permute-done | bytes 2621472 | tf_op jit(solution)/shard_map/ppermute | solution.py:24
  38.4 0.2 fusion
  38.7 0.1 collective-permute-start.6
  38.8 0.1 slice.24
  38.9 7.3 %collective-permute-start.1 = (f32[512,512]{1,0:T(8,128)S(1)}, f32[512,512]{1,0:T(8,128)S(1)}, u32[]{:S(2)}, u32[]{:S(2)}) collective-permute-start(f32[512,512]{1,0:T(8,128)S(1)} %slice.24), channel_id=1, source_target_pairs={{1,2},{2,1},{3,4},{4,3},{5,6},{6,5},{7,8},{8,7},{9,10},{10,9},{11,... | collective-permute-start | bytes 3145736 | tf_op jit(solution)/shard_map/ppermute | solution.py:24
  46.2 0.0 collective-permute-start.5
  46.2 0.5 collective-permute-start.4
  46.7 0.0 collective-permute-done.6.refs_14_
  46.7 0.0 collective-permute-start.3
  46.7 1.6 %collective-permute-done.5.refs_11_ = f32[128,1280]{1,0:T(8,128)S(1)} collective-permute-done((f32[128,1280]{1,0:T(8,128)S(1)}, f32[128,1280]{1,0:T(8,128)S(1)}, u32[]{:S(2)}, u32[]{:S(2)}) %collective-permute-start.5) | collective-permute-done | bytes 655392 | tf_op jit(solution)/shard_map/ppermute | solution.py:24
  48.3 0.9 %collective-permute-done.4.refs_8_ = f32[128,1280]{1,0:T(8,128)S(1)} collective-permute-done((f32[128,1280]{1,0:T(8,128)S(1)}, f32[128,1280]{1,0:T(8,128)S(1)}, u32[]{:S(2)}, u32[]{:S(2)}) %collective-permute-start.4) | collective-permute-done | bytes 655392 | tf_op jit(solution)/shard_map/ppermute | solution.py:24
  49.2 0.9 %collective-permute-done.3.refs_5_ = f32[128,1280]{1,0:T(8,128)S(1)} collective-permute-done((f32[128,1280]{1,0:T(8,128)S(1)}, f32[128,1280]{1,0:T(8,128)S(1)}, u32[]{:S(2)}, u32[]{:S(2)}) %collective-permute-start.3) | collective-permute-done | bytes 655392 | tf_op jit(solution)/shard_map/ppermute | solution.py:24
  50.2 8.0 %middle.1.refs_3_ = f32[512,1280]{1,0:T(8,128)S(1)} custom-call(bf16[5,512,512]{2,1,0:T(8,128)(2,1)S(1)} %get-tuple-element.9.refs_0_.refs_3_.refs_6_.refs_9_.refs_12_, bf16[5,512,512]{2,1,0:T(8,128)(2,1)S(1)} %get-tuple-element.10.refs_1_.refs_4_.refs_7_.refs_10_.refs_13_, f32[512,1280]{1,0:T(8,128)S(1)} %collective-permute-done.2.refs_2_, ...), custom_call_target="tpu_custom_call" | custom-call | flops 1 | bytes 1 | tf_op jit(solution)/shard_map/middle/pallas_call | solution.py:93
  58.1 0.0 collective-permute-done.7.refs_2_
  58.1 2.4 %last0.1.refs_4_ = f32[512,1280]{1,0:T(8,128)} custom-call(bf16[5,512,512]{2,1,0:T(8,128)(2,1)S(1)} %get-tuple-element.9.refs_0_.refs_3_.refs_6_.refs_9_.refs_12_, bf16[5,512,512]{2,1,0:T(8,128)(2,1)S(1)} %get-tuple-element.10.refs_1_.refs_4_.refs_7_.refs_10_.refs_13_, f32[512,768]{1,0:T(8,128)S(1)} %collective-permute-done.7.refs_2_, ...), custom_call_target="tpu_custom_call" | custom-call | flops 1 | bytes 1 | tf_op jit(solution)/shard_map/last0/pallas_call | solution.py:132
  60.6 6.0 %collective-permute-done.1.refs_2_ = f32[512,512]{1,0:T(8,128)S(1)} collective-permute-done((f32[512,512]{1,0:T(8,128)S(1)}, f32[512,512]{1,0:T(8,128)S(1)}, u32[]{:S(2)}, u32[]{:S(2)}) %collective-permute-start.1) | collective-permute-done | bytes 1048608 | tf_op jit(solution)/shard_map/ppermute | solution.py:24
  66.5 2.0 %last1.1 = f32[512,1280]{1,0:T(8,128)} custom-call(bf16[5,512,512]{2,1,0:T(8,128)(2,1)S(1)} %get-tuple-element.9.refs_0_.refs_3_.refs_6_.refs_9_.refs_12_, bf16[5,512,512]{2,1,0:T(8,128)(2,1)S(1)} %get-tuple-element.10.refs_1_.refs_4_.refs_7_.refs_10_.refs_13_, f32[512,512]{1,0:T(8,128)S(1)} %collective-permute-done.1.refs_2_, ...), custom_call_target="tpu_custom_call", output_to_operand_aliasing={{}: (4, {})} | custom-call | flops 1 | bytes 1 | tf_op jit(solution)/shard_map/last1/pallas_call | solution.py:132
Async XLA Ops:
  0.0 13.9 %collective-permute-start = (f32[512,1280]{1,0:T(8,128)}, f32[512,1280]{1,0:T(8,128)S(1)}, u32[]{:S(2)}, u32[]{:S(2)}) collective-permute-start(f32[512,1280]{1,0:T(8,128)} %refs_2_.1), channel_id=1, source_target_pairs={{0,1},{1,0},{2,3},{3,2},{4,5},{5,4},{6,7},{7,6},{8,9},{9,8},{10,11... | collective-permute-start | bytes 7864328 | tf_op jit(solution)/shard_map/ppermute | solution.py:24
  0.0 38.4 %collective-permute-start.2 = (f32[512,1280]{1,0:T(8,128)}, f32[512,1280]{1,0:T(8,128)S(1)}, u32[]{:S(2)}, u32[]{:S(2)}) collective-permute-start(f32[512,1280]{1,0:T(8,128)} %refs_2_.1), channel_id=1, source_target_pairs={{1,2},{2,1},{3,4},{4,3},{5,6},{6,5},{7,8},{8,7},{9,10},{10,9},{11,... | collective-permute-start | bytes 7864328 | tf_op jit(solution)/shard_map/ppermute | solution.py:24
  8.9 2.3 %copy-start = (f32[512,2176]{1,0:T(8,128)S(1)}, f32[512,2176]{1,0:T(8,128)}, u32[]{:S(2)}) copy-start(f32[512,2176]{1,0:T(8,128)} %v_ref.1) | copy-start | bytes 13369348
  11.1 0.7 copy-start.3
  11.8 2.3 %copy-start.2 = (f32[512,1280]{1,0:T(8,128)S(1)}, f32[512,1280]{1,0:T(8,128)}, u32[]{:S(2)}) copy-start(f32[512,1280]{1,0:T(8,128)} %refs_2_.1) | copy-start | bytes 7864324
  13.9 1.7 %copy-start.1 = (f32[512,1280]{1,0:T(8,128)S(1)}, f32[512,1280]{1,0:T(8,128)}, u32[]{:S(2)}) copy-start(f32[512,1280]{1,0:T(8,128)} %refs_6_.1) | copy-start | bytes 7864324
  14.1 44.1 %collective-permute-start.7 = (f32[512,768]{1,0:T(8,128)S(1)}, f32[512,768]{1,0:T(8,128)S(1)}, u32[]{:S(2)}, u32[]{:S(2)}) collective-permute-start(f32[512,768]{1,0:T(8,128)S(1)} %slice.25), channel_id=1, source_target_pairs={{1,2},{2,1},{3,4},{4,3},{5,6},{6,5},{7,8},{8,7},{9,10},{10,9},{11,... | collective-permute-start | bytes 4718600 | tf_op jit(solution)/shard_map/ppermute | solution.py:24
  38.7 8.0 %collective-permute-start.6 = (f32[128,1280]{1,0:T(8,128)S(1)}, f32[128,1280]{1,0:T(8,128)S(1)}, u32[]{:S(2)}, u32[]{:S(2)}) collective-permute-start(f32[128,1280]{1,0:T(8,128)S(1)} %get-tuple-element.13), channel_id=1, source_target_pairs={{0,1},{1,0},{2,3},{3,2},{4,5},{5,4},{6,7},{7,6},{8,9},{9,8},{10,11... | collective-permute-start | bytes 1966088 | tf_op jit(solution)/shard_map/ppermute | solution.py:24
  38.9 27.6 %collective-permute-start.1 = (f32[512,512]{1,0:T(8,128)S(1)}, f32[512,512]{1,0:T(8,128)S(1)}, u32[]{:S(2)}, u32[]{:S(2)}) collective-permute-start(f32[512,512]{1,0:T(8,128)S(1)} %slice.24), channel_id=1, source_target_pairs={{1,2},{2,1},{3,4},{4,3},{5,6},{6,5},{7,8},{8,7},{9,10},{10,9},{11,... | collective-permute-start | bytes 3145736 | tf_op jit(solution)/shard_map/ppermute | solution.py:24
  46.2 2.1 %collective-permute-start.5 = (f32[128,1280]{1,0:T(8,128)S(1)}, f32[128,1280]{1,0:T(8,128)S(1)}, u32[]{:S(2)}, u32[]{:S(2)}) collective-permute-start(f32[128,1280]{1,0:T(8,128)S(1)} %get-tuple-element.14), channel_id=1, source_target_pairs={{0,1},{1,0},{2,3},{3,2},{4,5},{5,4},{6,7},{7,6},{8,9},{9,8},{10,11... | collective-permute-start | bytes 1966088 | tf_op jit(solution)/shard_map/ppermute | solution.py:24
  46.2 3.0 %collective-permute-start.4 = (f32[128,1280]{1,0:T(8,128)S(1)}, f32[128,1280]{1,0:T(8,128)S(1)}, u32[]{:S(2)}, u32[]{:S(2)}) collective-permute-start(f32[128,1280]{1,0:T(8,128)S(1)} %get-tuple-element.15), channel_id=1, source_target_pairs={{0,1},{1,0},{2,3},{3,2},{4,5},{5,4},{6,7},{7,6},{8,9},{9,8},{10,11... | collective-permute-start | bytes 1966088 | tf_op jit(solution)/shard_map/ppermute | solution.py:24
  46.7 3.5 %collective-permute-start.3 = (f32[128,1280]{1,0:T(8,128)S(1)}, f32[128,1280]{1,0:T(8,128)S(1)}, u32[]{:S(2)}, u32[]{:S(2)}) collective-permute-start(f32[128,1280]{1,0:T(8,128)S(1)} %get-tuple-element.16), channel_id=1, source_target_pairs={{0,1},{1,0},{2,3},{3,2},{4,5},{5,4},{6,7},{7,6},{8,9},{9,8},{10,11... | collective-permute-start | bytes 1966088 | tf_op jit(solution)/shard_map/ppermute | solution.py:24

commit v2 on v1

--- a/solution.py
+++ b/solution.py
@@ -146,14 +146,16 @@
     rows, width = amplitudes.shape
     facing = exchange(amplitudes, 1)
     high, low = align(integrals, tile_pattern)
-    partner = exchange(amplitudes, 0)
-    cuts = [0, 768, 1280]
+    n = rows // 2
+    pieces = [exchange(amplitudes[i : i + n], 0) for i in range(0, rows, n)]
+    partner = jnp.concatenate(pieces, 0)
+    cuts = [0, 1024, 1280]
     beyond = [exchange(partner[:, a:b], 1) for a, b in zip(cuts, cuts[1:])]
     acc = add_products(residual_in, high, low, [(OWN, 0, amplitudes), (PARTNER, 0, partner)], 256, "near")
     facing, acc = lax.optimization_barrier((facing, acc))
-    n = rows // 4
+    n = rows // 2
     beside = [exchange(facing[i : i + n], 0) for i in range(0, rows, n)]
-    parts = [(FACING, 0, facing)] + [(BESIDE, i, block) for i, block in enumerate(beside)]
+    parts = [(FACING, 0, facing), (BESIDE, 0, jnp.concatenate(beside, 0))]
     acc = add_products(acc, high, low, parts, 256, "middle")
     out = None
     for i, block in enumerate(beyond):

time: 68.7 us -> 67.3 us (0.980)
  Pallas kernels: 20.1 us -> 17.7 us
  waiting for transfers between devices: 26.5 us -> 27.9 us
  local copies, waits for them, and re-layouts: 4.93 us -> 3.64 us
  starting transfers between devices: 16.8 us -> 17.7 us
    unnamed x8 -> x9, local copies, waits for them, and re-layouts: 4.45 us -> 1.17 us
    pallas_call x2, Pallas kernels: 13.6 us -> 11.3 us  [add_products(): pl.pallas_call(functools.partial(add_kernel, n), grid=(width // cols,), i...]
    slice x0 -> x1, local copies, waits for them, and re-layouts: none -> 1.88 us  [per_device(): pieces = [exchange(amplitudes[i:i + n], 0) for i in range(0, rows, n)]]
    ppermute x8 -> x7, waiting for transfers between devices: 26.5 us -> 27.9 us  [exchange(): return lax.ppermute(value, AXIS, pairs)]
    ppermute x8 -> x7, starting transfers between devices: 16.8 us -> 17.7 us  [exchange(): return lax.ppermute(value, AXIS, pairs)]
  transfers between devices with their start and end apart: 8 -> 7, of which waited for: 5 -> 5; matrix products, arithmetic and copies ran while one was open for 1% -> 4% of each run, Pallas kernels for 26% -> 24%
where the time goes in v2:
time: 67.3 us; the launch traced here: 67.2 us
  waiting for transfers between devices  27.9 us (41%)
  starting transfers between devices  17.7 us (26%)
  Pallas kernels  17.7 us (26%)
  local copies, waits for them, and re-layouts  3.64 us (5%)
    ppermute x7, waiting for transfers between devices, exchange(): return lax.ppermute(value, AXIS, pairs)  27.9 us
    ppermute x7, starting transfers between devices, exchange(): return lax.ppermute(value, AXIS, pairs)  17.7 us
    pallas_call x2, Pallas kernels, add_products(): pl.pallas_call(functools.partial(add_kernel, n), grid=(width // cols,), i...  11.3 us
    pallas_call x2, Pallas kernels, add_last(): pl.pallas_call(functools.partial(last_kernel, start, step), in_specs=spec...  4.28 us
    pallas_call x1, Pallas kernels, align(): pl.pallas_call(functools.partial(align_kernel, tiles), grid=(tiles,), in_...  2.08 us
    slice x1, local copies, waits for them, and re-layouts, per_device(): pieces = [exchange(amplitudes[i:i + n], 0) for i in range(0, rows, n)]  1.88 us
  transfers between devices with their start and end apart: 7, of which 5 were waited for; matrix products, arithmetic and copies ran while one was open for 4% of the time, Pallas kernels for 24%

profile of v2, /device:TPU:0, one launch (start us, length us, event | category | flops | bytes accessed | tf_op | source)
XLA Modules:
  0.0 67.2 jit_solution(1261025947168777072)
XLA Ops:
  0.0 0.0 copy-start.3
  0.0 0.0 copy-start.1
  0.0 8.2 %collective-permute-start.3 = (f32[512,1280]{1,0:T(8,128)}, f32[512,1280]{1,0:T(8,128)S(1)}, u32[]{:S(2)}, u32[]{:S(2)}) collective-permute-start(f32[512,1280]{1,0:T(8,128)} %refs_2_.1), channel_id=1, source_target_pairs={{1,2},{2,1},{3,4},{4,3},{5,6},{6,5},{7,8},{8,7},{9,10},{10,9},{11,... | collective-permute-start | bytes 7864328 | tf_op jit(solution)/shard_map/ppermute | solution.py:24
  8.2 1.9 %fusion.1 = (f32[256,1280]{1,0:T(8,128)S(1)}, f32[256,1280]{1,0:T(8,128)S(1)}) fusion(f32[512,1280]{1,0:T(8,128)} %refs_2_.1), kind=kLoop, calls=%fused_computation.4 | loop fusion | bytes 5242880 | tf_op jit(solution)/shard_map/slice | solution.py:150
  10.1 0.1 collective-permute-start
  10.2 0.5 collective-permute-start.1
  10.7 0.0 copy-done.3
  10.7 0.0 copy-done.1
  10.7 2.1 %align.1 = (bf16[5,512,512]{2,1,0:T(8,128)(2,1)S(1)}, bf16[5,512,512]{2,1,0:T(8,128)(2,1)S(1)}) custom-call(s32[4,17]{1,0:T(4,128)S(1)} %copy-done.3, f32[512,2176]{1,0:T(8,128)S(1)} %copy-done.1), custom_call_target="tpu_custom_call" | custom-call | flops 2621440 | bytes 10000000 | tf_op jit(solution)/shard_map/align/pallas_call | solution.py:55
  12.8 0.4 collective-permute-done
  13.2 0.1 constant_dynamic-update-slice_fusion.1
  13.3 1.8 %collective-permute-done.1 = f32[256,1280]{1,0:T(8,128)S(1)} collective-permute-done((f32[256,1280]{1,0:T(8,128)S(1)}, f32[256,1280]{1,0:T(8,128)S(1)}, u32[]{:S(2)}, u32[]{:S(2)}) %collective-permute-start.1) | collective-permute-done | bytes 1310752 | tf_op jit(solution)/shard_map/ppermute | solution.py:24
  15.1 0.0 copy-start.2
  15.1 0.1 constant_dynamic-update-slice_fusion.refs_5_
  15.2 0.0 copy-start
  15.2 0.3 slice.25
  15.5 1.1 %collective-permute-start.6 = (f32[512,1024]{1,0:T(8,128)S(1)}, f32[512,1024]{1,0:T(8,128)S(1)}, u32[]{:S(2)}, u32[]{:S(2)}) collective-permute-start(f32[512,1024]{1,0:T(8,128)S(1)} %slice.25), channel_id=1, source_target_pairs={{1,2},{2,1},{3,4},{4,3},{5,6},{6,5},{7,8},{8,7},{9,10},{10,9},{11,... | collective-permute-start | bytes 6291464 | tf_op jit(solution)/shard_map/ppermute | solution.py:24
  16.6 0.3 copy-done.2
  16.8 0.8 %copy-done = f32[512,1280]{1,0:T(8,128)S(1)} copy-done((f32[512,1280]{1,0:T(8,128)S(1)}, f32[512,1280]{1,0:T(8,128)}, u32[]{:S(2)}) %copy-start) | copy-done | bytes 2621464
  17.6 5.6 %near.1.refs_6_ = f32[512,1280]{1,0:T(8,128)S(1)} custom-call(bf16[5,512,512]{2,1,0:T(8,128)(2,1)S(1)} %get-tuple-element.9.refs_0_.refs_3_, bf16[5,512,512]{2,1,0:T(8,128)(2,1)S(1)} %get-tuple-element.10.refs_1_.refs_4_, f32[512,1280]{1,0:T(8,128)S(1)} %copy-done, bf16[5,512,512]{2,1,0:T(8,128)(2,1)S(1)} %get-tuple-element.9.refs_0_.refs_3_, ...), custom_call_target="tpu_custom_call" | custom-call | flops 1 | bytes 1 | tf_op jit(solution)/shard_map/near/pallas_call | solution.py:93
  23.3 14.5 %collective-permute-done.3.refs_2_ = f32[512,1280]{1,0:T(8,128)S(1)} collective-permute-done((f32[512,1280]{1,0:T(8,128)}, f32[512,1280]{1,0:T(8,128)S(1)}, u32[]{:S(2)}, u32[]{:S(2)}) %collective-permute-start.3) | collective-permute-done | bytes 2621472 | tf_op jit(solution)/shard_map/ppermute | solution.py:24
  37.8 0.2 fusion
  37.9 0.1 collective-permute-start.4
  38.0 0.5 collective-permute-start.5
  38.6 7.3 %collective-permute-start.2 = (f32[512,256]{1,0:T(8,128)S(1)}, f32[512,256]{1,0:T(8,128)S(1)}, u32[]{:S(2)}, u32[]{:S(2)}) collective-permute-start(f32[512,256]{1,0:T(8,128)S(1)} %slice.24), channel_id=1, source_target_pairs={{1,2},{2,1},{3,4},{4,3},{5,6},{6,5},{7,8},{8,7},{9,10},{10,9},{11,... | collective-permute-start | bytes 1572872 | tf_op jit(solution)/shard_map/ppermute | solution.py:24
  45.8 0.0 collective-permute-done.4
  45.8 0.0 collective-permute-done.5
  45.8 0.2 pad_maximum_fusion.refs_5_
  46.0 5.7 %middle.1.refs_3_ = f32[512,1280]{1,0:T(8,128)S(1)} custom-call(bf16[5,512,512]{2,1,0:T(8,128)(2,1)S(1)} %get-tuple-element.9.refs_0_.refs_3_, bf16[5,512,512]{2,1,0:T(8,128)(2,1)S(1)} %get-tuple-element.10.refs_1_.refs_4_, f32[512,1280]{1,0:T(8,128)S(1)} %collective-permute-done.3.refs_2_, bf16[5,512,512]{2,1,0:T(8,128)(2,1)S(1)} %get-tuple-element.9.refs_0_.refs_3_, ...), custom_call_target="tpu_custom_call" | custom-call | flops 1 | bytes 1 | tf_op jit(solution)/shard_map/middle/pallas_call | solution.py:93
  51.7 8.6 %collective-permute-done.6.refs_2_ = f32[512,1024]{1,0:T(8,128)S(1)} collective-permute-done((f32[512,1024]{1,0:T(8,128)S(1)}, f32[512,1024]{1,0:T(8,128)S(1)}, u32[]{:S(2)}, u32[]{:S(2)}) %collective-permute-start.6) | collective-permute-done | bytes 2097184 | tf_op jit(solution)/shard_map/ppermute | solution.py:24
  60.2 2.9 %last0.1.refs_4_ = f32[512,1280]{1,0:T(8,128)} custom-call(bf16[5,512,512]{2,1,0:T(8,128)(2,1)S(1)} %get-tuple-element.9.refs_0_.refs_3_, bf16[5,512,512]{2,1,0:T(8,128)(2,1)S(1)} %get-tuple-element.10.refs_1_.refs_4_, f32[512,1024]{1,0:T(8,128)S(1)} %collective-permute-done.6.refs_2_, f32[512,1280]{1,0:T(8,128)S(1)} %middle.1.refs_3_), custom_call_target="tpu_custom_call" | custom-call | flops 1 | bytes 1 | tf_op jit(solution)/shard_map/last0/pallas_call | solution.py:132
  63.1 2.7 %collective-permute-done.2.refs_2_ = f32[512,256]{1,0:T(8,128)S(1)} collective-permute-done((f32[512,256]{1,0:T(8,128)S(1)}, f32[512,256]{1,0:T(8,128)S(1)}, u32[]{:S(2)}, u32[]{:S(2)}) %collective-permute-start.2) | collective-permute-done | bytes 524320 | tf_op jit(solution)/shard_map/ppermute | solution.py:24
  65.8 1.4 %last1.1 = f32[512,1280]{1,0:T(8,128)} custom-call(bf16[5,512,512]{2,1,0:T(8,128)(2,1)S(1)} %get-tuple-element.9.refs_0_.refs_3_, bf16[5,512,512]{2,1,0:T(8,128)(2,1)S(1)} %get-tuple-element.10.refs_1_.refs_4_, f32[512,256]{1,0:T(8,128)S(1)} %collective-permute-done.2.refs_2_, f32[512,1280]{1,0:T(8,128)S(1)} %middle.1.refs_3_, ...), custom_call_target="tpu_custom_call", output_to_operand_aliasing={{}: (4, {})} | custom-call | flops 1 | bytes 1 | tf_op jit(solution)/shard_map/last1/pallas_call | solution.py:132
  (1 shorter events, 0.0 us)
Async XLA Ops:
  0.0 10.7 %copy-start.3 = (s32[4,17]{1,0:T(4,128)S(1)}, s32[4,17]{1,0:T(4,128)}, u32[]{:S(2)}) copy-start(s32[4,17]{1,0:T(4,128)} %pattern_ref.1) | copy-start | bytes 820
  0.0 10.7 %copy-start.1 = (f32[512,2176]{1,0:T(8,128)S(1)}, f32[512,2176]{1,0:T(8,128)}, u32[]{:S(2)}) copy-start(f32[512,2176]{1,0:T(8,128)} %v_ref.1) | copy-start | bytes 13369348
  0.0 37.8 %collective-permute-start.3 = (f32[512,1280]{1,0:T(8,128)}, f32[512,1280]{1,0:T(8,128)S(1)}, u32[]{:S(2)}, u32[]{:S(2)}) collective-permute-start(f32[512,1280]{1,0:T(8,128)} %refs_2_.1), channel_id=1, source_target_pairs={{1,2},{2,1},{3,4},{4,3},{5,6},{6,5},{7,8},{8,7},{9,10},{10,9},{11,... | collective-permute-start | bytes 7864328 | tf_op jit(solution)/shard_map/ppermute | solution.py:24
  10.1 3.1 %collective-permute-start = (f32[256,1280]{1,0:T(8,128)S(1)}, f32[256,1280]{1,0:T(8,128)S(1)}, u32[]{:S(2)}, u32[]{:S(2)}) collective-permute-start(f32[256,1280]{1,0:T(8,128)S(1)} %get-tuple-element.16), channel_id=1, source_target_pairs={{0,1},{1,0},{2,3},{3,2},{4,5},{5,4},{6,7},{7,6},{8,9},{9,8},{10,11... | collective-permute-start | bytes 3932168 | tf_op jit(solution)/shard_map/ppermute | solution.py:24
  10.2 4.9 %collective-permute-start.1 = (f32[256,1280]{1,0:T(8,128)S(1)}, f32[256,1280]{1,0:T(8,128)S(1)}, u32[]{:S(2)}, u32[]{:S(2)}) collective-permute-start(f32[256,1280]{1,0:T(8,128)S(1)} %get-tuple-element.15), channel_id=1, source_target_pairs={{0,1},{1,0},{2,3},{3,2},{4,5},{5,4},{6,7},{7,6},{8,9},{9,8},{10,11... | collective-permute-start | bytes 3932168 | tf_op jit(solution)/shard_map/ppermute | solution.py:24
  15.1 1.7 %copy-start.2 = (f32[512,1280]{1,0:T(8,128)S(1)}, f32[512,1280]{1,0:T(8,128)}, u32[]{:S(2)}) copy-start(f32[512,1280]{1,0:T(8,128)} %refs_6_.1) | copy-start | bytes 7864324
  15.2 2.5 %copy-start = (f32[512,1280]{1,0:T(8,128)S(1)}, f32[512,1280]{1,0:T(8,128)}, u32[]{:S(2)}) copy-start(f32[512,1280]{1,0:T(8,128)} %refs_2_.1) | copy-start | bytes 7864324
  15.5 44.7 %collective-permute-start.6 = (f32[512,1024]{1,0:T(8,128)S(1)}, f32[512,1024]{1,0:T(8,128)S(1)}, u32[]{:S(2)}, u32[]{:S(2)}) collective-permute-start(f32[512,1024]{1,0:T(8,128)S(1)} %slice.25), channel_id=1, source_target_pairs={{1,2},{2,1},{3,4},{4,3},{5,6},{6,5},{7,8},{8,7},{9,10},{10,9},{11,... | collective-permute-start | bytes 6291464 | tf_op jit(solution)/shard_map/ppermute | solution.py:24
  37.9 7.9 %collective-permute-start.4 = (f32[256,1280]{1,0:T(8,128)S(1)}, f32[256,1280]{1,0:T(8,128)S(1)}, u32[]{:S(2)}, u32[]{:S(2)}) collective-permute-start(f32[256,1280]{1,0:T(8,128)S(1)} %get-tuple-element.13), channel_id=1, source_target_pairs={{0,1},{1,0},{2,3},{3,2},{4,5},{5,4},{6,7},{7,6},{8,9},{9,8},{10,11... | collective-permute-start | bytes 3932168 | tf_op jit(solution)/shard_map/ppermute | solution.py:24
  38.0 7.8 %collective-permute-start.5 = (f32[256,1280]{1,0:T(8,128)S(1)}, f32[256,1280]{1,0:T(8,128)S(1)}, u32[]{:S(2)}, u32[]{:S(2)}) collective-permute-start(f32[256,1280]{1,0:T(8,128)S(1)} %get-tuple-element.14), channel_id=1, source_target_pairs={{0,1},{1,0},{2,3},{3,2},{4,5},{5,4},{6,7},{7,6},{8,9},{9,8},{10,11... | collective-permute-start | bytes 3932168 | tf_op jit(solution)/shard_map/ppermute | solution.py:24
  38.6 27.3 %collective-permute-start.2 = (f32[512,256]{1,0:T(8,128)S(1)}, f32[512,256]{1,0:T(8,128)S(1)}, u32[]{:S(2)}, u32[]{:S(2)}) collective-permute-start(f32[512,256]{1,0:T(8,128)S(1)} %slice.24), channel_id=1, source_target_pairs={{1,2},{2,1},{3,4},{4,3},{5,6},{6,5},{7,8},{8,7},{9,10},{10,9},{11,... | collective-permute-start | bytes 1572872 | tf_op jit(solution)/shard_map/ppermute | solution.py:24

commit v3 on v2

--- a/solution.py
+++ b/solution.py
@@ -102,14 +102,18 @@
     )(*args)
 
 
-def last_kernel(start, step, *refs):
-    high_ref, low_ref, block_ref, acc_ref = refs[:4]
+def last_kernel(start, step, count, *refs):
+    high_ref, low_ref, acc_ref = refs[:3]
+    block_refs = refs[3 : 3 + count]
     out_ref, stage, sems = refs[-3:]
     copies = []
-    for i in range(block_ref.shape[1] // step):
+    for i in range(stage.shape[1] // step):
         here = slice(i * step, i * step + step)
         there = slice(start + i * step, start + i * step + step)
-        th, tl = split(block_ref[:, here])
+        block = [ref[:, here] for ref in block_refs]
+        if count == 3:
+            block = [jnp.concatenate([block[0], block[1] + block[2]], 0)]
+        th, tl = split(block[0])
         vh, vl = high_ref[BEYOND], low_ref[BEYOND]
         dot = functools.partial(jnp.dot, preferred_element_type=jnp.float32)
         stage[:, here] = acc_ref[:, there] + (dot(vh, th) + (dot(vh, tl) + dot(vl, th)))
@@ -119,18 +123,18 @@
         copy.wait()
 
 
-def add_last(acc, high, low, block, start, out, name):
-    rows, width = block.shape
+def add_last(acc, high, low, blocks, start, out, name):
+    rows, width = acc.shape[0], blocks[0].shape[1]
     step = 256
-    args = [high, low, block, acc]
-    specs = [pl.BlockSpec(memory_space=pltpu.VMEM)] * 4
+    args = [high, low, acc, *blocks]
+    specs = [pl.BlockSpec(memory_space=pltpu.VMEM)] * len(args)
     aliases = {}
     if out is not None:
         aliases = {len(args): 0}
         args.append(out)
         specs.append(pl.BlockSpec(memory_space=pl.ANY))
     return pl.pallas_call(
-        functools.partial(last_kernel, start, step),
+        functools.partial(last_kernel, start, step, len(blocks)),
         in_specs=specs,
         out_specs=pl.BlockSpec(memory_space=pl.ANY),
         out_shape=jax.ShapeDtypeStruct(acc.shape, acc.dtype),
@@ -142,25 +146,42 @@
     )(*args)
 
 
+def hops(count):
+    facing = [(i, (i + 1 if i % 2 else i - 1) % count) for i in range(count)]
+    far = [pair for pair in facing if {i // 64 for i in pair} != {pair[0] // 64}]
+    return facing, far
+
+
 def per_device(integrals, tile_pattern, amplitudes, residual_in):
     rows, width = amplitudes.shape
+    count = lax.axis_size(AXIS)
+    pairs, far = hops(count)
+    near = [pair for pair in pairs if pair not in far]
+    cut, kept = 1024, rows - 128
     facing = exchange(amplitudes, 1)
     high, low = align(integrals, tile_pattern)
     n = rows // 2
     pieces = [exchange(amplitudes[i : i + n], 0) for i in range(0, rows, n)]
     partner = jnp.concatenate(pieces, 0)
-    cuts = [0, 1024, 1280]
-    beyond = [exchange(partner[:, a:b], 1) for a, b in zip(cuts, cuts[1:])]
+    most = exchange(partner[:, :cut], 1)
+    rest = exchange(partner[:kept, cut:], 1)
+    slab = lax.ppermute(partner[kept:, cut:], AXIS, near)
+    out, back = [], []
+    for source, target in far:
+        holder = source ^ 1
+        relay = (holder + 16 if source % 2 else holder - 16) % count
+        out.append((holder, relay))
+        back.append((relay, target))
+    held = lax.ppermute(amplitudes[kept:, cut:], AXIS, out)
+    relayed = lax.ppermute(held, AXIS, back)
     acc = add_products(residual_in, high, low, [(OWN, 0, amplitudes), (PARTNER, 0, partner)], 256, "near")
     facing, acc = lax.optimization_barrier((facing, acc))
     n = rows // 2
     beside = [exchange(facing[i : i + n], 0) for i in range(0, rows, n)]
     parts = [(FACING, 0, facing), (BESIDE, 0, jnp.concatenate(beside, 0))]
     acc = add_products(acc, high, low, parts, 256, "middle")
-    out = None
-    for i, block in enumerate(beyond):
-        out = add_last(acc, high, low, block, cuts[i], out, "last%d" % i)
-    return out
+    result = add_last(acc, high, low, [most], 0, None, "last0")
+    return add_last(acc, high, low, [rest, slab, relayed], cut, result, "last1")
 
 
 def solution(mesh):

time: 67.3 us -> 66 us (0.981)
  waiting for transfers between devices: 27.9 us -> 23.8 us
  starting transfers between devices: 17.7 us -> 20.3 us
    ppermute x7, waiting for transfers between devices: 27.9 us -> 23.8 us  [exchange(): return lax.ppermute(value, AXIS, pairs)]
    ppermute x0 -> x3, starting transfers between devices: none -> 2.62 us  [the longest x1 1.28 us: per_device(): relayed = lax.ppermute(held, AXIS, back)]
  transfers between devices with their start and end apart: 7 -> 10, of which waited for: 5 -> 5; matrix products, arithmetic and copies ran while one was open for 4% -> 4% of each run, Pallas kernels for 24% -> 25%
where the time goes in v3:
time: 66 us; the launch traced here: 65.8 us
  waiting for transfers between devices  23.8 us (36%)
  starting transfers between devices  20.3 us (31%)
  Pallas kernels  17.7 us (27%)
  local copies, waits for them, and re-layouts  3.65 us (6%)
    ppermute x7, waiting for transfers between devices, exchange(): return lax.ppermute(value, AXIS, pairs)  23.8 us
    ppermute x7, starting transfers between devices, exchange(): return lax.ppermute(value, AXIS, pairs)  17.7 us
    pallas_call x2, Pallas kernels, add_products(): pl.pallas_call(functools.partial(add_kernel, n), grid=(width // cols,), i...  11.3 us
    pallas_call x2, Pallas kernels, add_last(): pl.pallas_call(functools.partial(last_kernel, start, step, len(blocks)),...  4.28 us
    pallas_call x1, Pallas kernels, align(): pl.pallas_call(functools.partial(align_kernel, tiles), grid=(tiles,), in_...  2.08 us
    slice x1, local copies, waits for them, and re-layouts, per_device(): pieces = [exchange(amplitudes[i:i + n], 0) for i in range(0, rows, n)]  1.88 us
  transfers between devices with their start and end apart: 10, of which 5 were waited for; matrix products, arithmetic and copies ran while one was open for 4% of the time, Pallas kernels for 25%

profile of v3, /device:TPU:0, one launch (start us, length us, event | category | flops | bytes accessed | tf_op | source)
XLA Modules:
  0.0 65.8 jit_solution(3860337375655170136)
XLA Ops:
  0.0 0.0 copy-start.3
  0.0 0.0 copy-start.1
  0.0 8.2 %collective-permute-start = (f32[512,1280]{1,0:T(8,128)}, f32[512,1280]{1,0:T(8,128)S(1)}, u32[]{:S(2)}, u32[]{:S(2)}) collective-permute-start(f32[512,1280]{1,0:T(8,128)} %refs_2_.1), channel_id=1, source_target_pairs={{1,2},{2,1},{3,4},{4,3},{5,6},{6,5},{7,8},{8,7},{9,10},{10,9},{11,... | collective-permute-start | bytes 7864328 | tf_op jit(solution)/shard_map/ppermute | solution.py:24
  8.2 1.9 %fusion.1 = (f32[256,1280]{1,0:T(8,128)S(1)}, f32[256,1280]{1,0:T(8,128)S(1)}) fusion(f32[512,1280]{1,0:T(8,128)} %refs_2_.1), kind=kLoop, calls=%fused_computation.4 | loop fusion | bytes 5242880 | tf_op jit(solution)/shard_map/slice | solution.py:164
  10.1 0.1 collective-permute-start.1
  10.2 0.5 collective-permute-start.2
  10.7 0.0 copy-done.3
  10.7 0.0 copy-done.1
  10.7 2.1 %align.1 = (bf16[5,512,512]{2,1,0:T(8,128)(2,1)S(1)}, bf16[5,512,512]{2,1,0:T(8,128)(2,1)S(1)}) custom-call(s32[4,17]{1,0:T(4,128)S(1)} %copy-done.3, f32[512,2176]{1,0:T(8,128)S(1)} %copy-done.1), custom_call_target="tpu_custom_call" | custom-call | flops 2621440 | bytes 10000000 | tf_op jit(solution)/shard_map/align/pallas_call | solution.py:55
  12.8 0.4 collective-permute-done.1
  13.2 0.1 constant_dynamic-update-slice_fusion.1
  13.3 1.8 %collective-permute-done.2 = f32[256,1280]{1,0:T(8,128)S(1)} collective-permute-done((f32[256,1280]{1,0:T(8,128)S(1)}, f32[256,1280]{1,0:T(8,128)S(1)}, u32[]{:S(2)}, u32[]{:S(2)}) %collective-permute-start.2) | collective-permute-done | bytes 1310752 | tf_op jit(solution)/shard_map/ppermute | solution.py:24
  15.1 0.0 copy-start.2
  15.1 0.1 constant_dynamic-update-slice_fusion.refs_5_
  15.2 0.0 copy-start
  15.2 0.3 slice.34
  15.5 1.1 %collective-permute-start.9 = (f32[512,1024]{1,0:T(8,128)S(1)}, f32[512,1024]{1,0:T(8,128)S(1)}, u32[]{:S(2)}, u32[]{:S(2)}) collective-permute-start(f32[512,1024]{1,0:T(8,128)S(1)} %slice.34), channel_id=1, source_target_pairs={{1,2},{2,1},{3,4},{4,3},{5,6},{6,5},{7,8},{8,7},{9,10},{10,9},{11,... | collective-permute-start | bytes 6291464 | tf_op jit(solution)/shard_map/ppermute | solution.py:24
  16.6 0.3 copy-done.2
  16.8 0.8 %copy-done = f32[512,1280]{1,0:T(8,128)S(1)} copy-done((f32[512,1280]{1,0:T(8,128)S(1)}, f32[512,1280]{1,0:T(8,128)}, u32[]{:S(2)}) %copy-start) | copy-done | bytes 2621464
  17.6 5.6 %near.1.refs_6_ = f32[512,1280]{1,0:T(8,128)S(1)} custom-call(bf16[5,512,512]{2,1,0:T(8,128)(2,1)S(1)} %get-tuple-element.9.refs_0_.refs_3_, bf16[5,512,512]{2,1,0:T(8,128)(2,1)S(1)} %get-tuple-element.10.refs_1_.refs_4_, f32[512,1280]{1,0:T(8,128)S(1)} %copy-done, bf16[5,512,512]{2,1,0:T(8,128)(2,1)S(1)} %get-tuple-element.9.refs_0_.refs_3_, ...), custom_call_target="tpu_custom_call" | custom-call | flops 1 | bytes 1 | tf_op jit(solution)/shard_map/near/pallas_call | solution.py:93
  23.3 14.5 %collective-permute-done.refs_2_ = f32[512,1280]{1,0:T(8,128)S(1)} collective-permute-done((f32[512,1280]{1,0:T(8,128)}, f32[512,1280]{1,0:T(8,128)S(1)}, u32[]{:S(2)}, u32[]{:S(2)}) %collective-permute-start) | collective-permute-done | bytes 2621472 | tf_op jit(solution)/shard_map/ppermute | solution.py:24
  37.8 0.2 fusion
  37.9 0.1 collective-permute-start.3
  38.0 0.5 collective-permute-start.4
  38.5 0.7 %collective-permute-start.7 = (f32[128,256]{1,0:T(8,128)S(1)}, f32[128,256]{1,0:T(8,128)S(1)}, u32[]{:S(2)}, u32[]{:S(2)}) collective-permute-start(f32[128,256]{1,0:T(8,128)S(1)} %slice.30), channel_id=1, source_target_pairs={{1,241},{62,78},{65,49},{126,142},{129,113},{190,206},{193,177},{2... | collective-permute-start | bytes 393224 | tf_op jit(solution)/shard_map/ppermute | solution.py:175
  39.3 7.3 %collective-permute-start.5 = (f32[384,256]{1,0:T(8,128)S(1)}, f32[384,256]{1,0:T(8,128)S(1)}, u32[]{:S(2)}, u32[]{:S(2)}) collective-permute-start(f32[384,256]{1,0:T(8,128)S(1)} %slice.32), channel_id=1, source_target_pairs={{1,2},{2,1},{3,4},{4,3},{5,6},{6,5},{7,8},{8,7},{9,10},{10,9},{11,... | collective-permute-start | bytes 1179656 | tf_op jit(solution)/shard_map/ppermute | solution.py:24
  46.5 0.0 collective-permute-done.7
  46.5 1.3 %collective-permute-start.8 = (f32[128,256]{1,0:T(8,128)S(1)}, f32[128,256]{1,0:T(8,128)S(1)}, u32[]{:S(2)}, u32[]{:S(2)}) collective-permute-start(f32[128,256]{1,0:T(8,128)S(1)} %collective-permute-done.7), channel_id=1, source_target_pairs={{241,255},{78,64},{49,63},{142,128},{113,127},{206,192},{177,191},... | collective-permute-start | bytes 393224 | tf_op jit(solution)/shard_map/ppermute | solution.py:176
  47.8 0.0 collective-permute-done.3
  47.8 0.7 %collective-permute-start.6 = (f32[128,256]{1,0:T(8,128)S(1)}, f32[128,256]{1,0:T(8,128)S(1)}, u32[]{:S(2)}, u32[]{:S(2)}) collective-permute-start(f32[128,256]{1,0:T(8,128)S(1)} %slice.33), channel_id=1, source_target_pairs={{1,2},{2,1},{3,4},{4,3},{5,6},{6,5},{7,8},{8,7},{9,10},{10,9},{11,... | collective-permute-start | bytes 393224 | tf_op jit(solution)/shard_map/ppermute | solution.py:168
  48.5 0.0 collective-permute-done.4
  48.5 0.2 pad_maximum_fusion.refs_5_
  48.7 5.7 %middle.1.refs_2_ = f32[512,1280]{1,0:T(8,128)S(1)} custom-call(bf16[5,512,512]{2,1,0:T(8,128)(2,1)S(1)} %get-tuple-element.9.refs_0_.refs_3_, bf16[5,512,512]{2,1,0:T(8,128)(2,1)S(1)} %get-tuple-element.10.refs_1_.refs_4_, f32[512,1280]{1,0:T(8,128)S(1)} %collective-permute-done.refs_2_, bf16[5,512,512]{2,1,0:T(8,128)(2,1)S(1)} %get-tuple-element.9.refs_0_.refs_3_, ...), custom_call_target="tpu_custom_call" | custom-call | flops 1 | bytes 1 | tf_op jit(solution)/shard_map/middle/pallas_call | solution.py:93
  54.4 5.9 %collective-permute-done.9.refs_3_ = f32[512,1024]{1,0:T(8,128)S(1)} collective-permute-done((f32[512,1024]{1,0:T(8,128)S(1)}, f32[512,1024]{1,0:T(8,128)S(1)}, u32[]{:S(2)}, u32[]{:S(2)}) %collective-permute-start.9) | collective-permute-done | bytes 2097184 | tf_op jit(solution)/shard_map/ppermute | solution.py:24
  60.2 2.9 %last0.1.refs_6_ = f32[512,1280]{1,0:T(8,128)} custom-call(bf16[5,512,512]{2,1,0:T(8,128)(2,1)S(1)} %get-tuple-element.9.refs_0_.refs_3_, bf16[5,512,512]{2,1,0:T(8,128)(2,1)S(1)} %get-tuple-element.10.refs_1_.refs_4_, f32[512,1280]{1,0:T(8,128)S(1)} %middle.1.refs_2_, f32[512,1024]{1,0:T(8,128)S(1)} %collective-permute-done.9.refs_3_), custom_call_target="tpu_custom_call" | custom-call | flops 1 | bytes 1 | tf_op jit(solution)/shard_map/last0/pallas_call | solution.py:136
  63.1 0.0 collective-permute-done.8.refs_5_
  63.1 0.0 collective-permute-done.6.refs_4_
  63.2 1.3 %collective-permute-done.5.refs_3_ = f32[384,256]{1,0:T(8,128)S(1)} collective-permute-done((f32[384,256]{1,0:T(8,128)S(1)}, f32[384,256]{1,0:T(8,128)S(1)}, u32[]{:S(2)}, u32[]{:S(2)}) %collective-permute-start.5) | collective-permute-done | bytes 393248 | tf_op jit(solution)/shard_map/ppermute | solution.py:24
  64.4 1.4 %last1.1 = f32[512,1280]{1,0:T(8,128)} custom-call(bf16[5,512,512]{2,1,0:T(8,128)(2,1)S(1)} %get-tuple-element.9.refs_0_.refs_3_, bf16[5,512,512]{2,1,0:T(8,128)(2,1)S(1)} %get-tuple-element.10.refs_1_.refs_4_, f32[512,1280]{1,0:T(8,128)S(1)} %middle.1.refs_2_, f32[384,256]{1,0:T(8,128)S(1)} %collective-permute-done.5.refs_3_, ...), custom_call_target="tpu_custom_call", output_to_operand_aliasing={{}: (6, {})} | custom-call | flops 1 | bytes 1 | tf_op jit(solution)/shard_map/last1/pallas_call | solution.py:136
  (3 shorter events, 0.0 us)
Async XLA Ops:
  0.0 10.7 %copy-start.3 = (s32[4,17]{1,0:T(4,128)S(1)}, s32[4,17]{1,0:T(4,128)}, u32[]{:S(2)}) copy-start(s32[4,17]{1,0:T(4,128)} %pattern_ref.1) | copy-start | bytes 820
  0.0 10.7 %copy-start.1 = (f32[512,2176]{1,0:T(8,128)S(1)}, f32[512,2176]{1,0:T(8,128)}, u32[]{:S(2)}) copy-start(f32[512,2176]{1,0:T(8,128)} %v_ref.1) | copy-start | bytes 13369348
  0.0 37.8 %collective-permute-start = (f32[512,1280]{1,0:T(8,128)}, f32[512,1280]{1,0:T(8,128)S(1)}, u32[]{:S(2)}, u32[]{:S(2)}) collective-permute-start(f32[512,1280]{1,0:T(8,128)} %refs_2_.1), channel_id=1, source_target_pairs={{1,2},{2,1},{3,4},{4,3},{5,6},{6,5},{7,8},{8,7},{9,10},{10,9},{11,... | collective-permute-start | bytes 7864328 | tf_op jit(solution)/shard_map/ppermute | solution.py:24
  10.1 3.1 %collective-permute-start.1 = (f32[256,1280]{1,0:T(8,128)S(1)}, f32[256,1280]{1,0:T(8,128)S(1)}, u32[]{:S(2)}, u32[]{:S(2)}) collective-permute-start(f32[256,1280]{1,0:T(8,128)S(1)} %get-tuple-element.16), channel_id=1, source_target_pairs={{0,1},{1,0},{2,3},{3,2},{4,5},{5,4},{6,7},{7,6},{8,9},{9,8},{10,11... | collective-permute-start | bytes 3932168 | tf_op jit(solution)/shard_map/ppermute | solution.py:24
  10.2 4.9 %collective-permute-start.2 = (f32[256,1280]{1,0:T(8,128)S(1)}, f32[256,1280]{1,0:T(8,128)S(1)}, u32[]{:S(2)}, u32[]{:S(2)}) collective-permute-start(f32[256,1280]{1,0:T(8,128)S(1)} %get-tuple-element.15), channel_id=1, source_target_pairs={{0,1},{1,0},{2,3},{3,2},{4,5},{5,4},{6,7},{7,6},{8,9},{9,8},{10,11... | collective-permute-start | bytes 3932168 | tf_op jit(solution)/shard_map/ppermute | solution.py:24
  15.1 1.7 %copy-start.2 = (f32[512,1280]{1,0:T(8,128)S(1)}, f32[512,1280]{1,0:T(8,128)}, u32[]{:S(2)}) copy-start(f32[512,1280]{1,0:T(8,128)} %refs_6_.1) | copy-start | bytes 7864324
  15.2 2.5 %copy-start = (f32[512,1280]{1,0:T(8,128)S(1)}, f32[512,1280]{1,0:T(8,128)}, u32[]{:S(2)}) copy-start(f32[512,1280]{1,0:T(8,128)} %refs_2_.1) | copy-start | bytes 7864324
  15.5 44.7 %collective-permute-start.9 = (f32[512,1024]{1,0:T(8,128)S(1)}, f32[512,1024]{1,0:T(8,128)S(1)}, u32[]{:S(2)}, u32[]{:S(2)}) collective-permute-start(f32[512,1024]{1,0:T(8,128)S(1)} %slice.34), channel_id=1, source_target_pairs={{1,2},{2,1},{3,4},{4,3},{5,6},{6,5},{7,8},{8,7},{9,10},{10,9},{11,... | collective-permute-start | bytes 6291464 | tf_op jit(solution)/shard_map/ppermute | solution.py:24
  37.9 9.9 %collective-permute-start.3 = (f32[256,1280]{1,0:T(8,128)S(1)}, f32[256,1280]{1,0:T(8,128)S(1)}, u32[]{:S(2)}, u32[]{:S(2)}) collective-permute-start(f32[256,1280]{1,0:T(8,128)S(1)} %get-tuple-element.13), channel_id=1, source_target_pairs={{0,1},{1,0},{2,3},{3,2},{4,5},{5,4},{6,7},{7,6},{8,9},{9,8},{10,11... | collective-permute-start | bytes 3932168 | tf_op jit(solution)/shard_map/ppermute | solution.py:24
  38.0 10.5 %collective-permute-start.4 = (f32[256,1280]{1,0:T(8,128)S(1)}, f32[256,1280]{1,0:T(8,128)S(1)}, u32[]{:S(2)}, u32[]{:S(2)}) collective-permute-start(f32[256,1280]{1,0:T(8,128)S(1)} %get-tuple-element.14), channel_id=1, source_target_pairs={{0,1},{1,0},{2,3},{3,2},{4,5},{5,4},{6,7},{7,6},{8,9},{9,8},{10,11... | collective-permute-start | bytes 3932168 | tf_op jit(solution)/shard_map/ppermute | solution.py:24
  38.5 8.0 %collective-permute-start.7 = (f32[128,256]{1,0:T(8,128)S(1)}, f32[128,256]{1,0:T(8,128)S(1)}, u32[]{:S(2)}, u32[]{:S(2)}) collective-permute-start(f32[128,256]{1,0:T(8,128)S(1)} %slice.30), channel_id=1, source_target_pairs={{1,241},{62,78},{65,49},{126,142},{129,113},{190,206},{193,177},{2... | collective-permute-start | bytes 393224 | tf_op jit(solution)/shard_map/ppermute | solution.py:175
  39.3 25.2 %collective-permute-start.5 = (f32[384,256]{1,0:T(8,128)S(1)}, f32[384,256]{1,0:T(8,128)S(1)}, u32[]{:S(2)}, u32[]{:S(2)}) collective-permute-start(f32[384,256]{1,0:T(8,128)S(1)} %slice.32), channel_id=1, source_target_pairs={{1,2},{2,1},{3,4},{4,3},{5,6},{6,5},{7,8},{8,7},{9,10},{10,9},{11,... | collective-permute-start | bytes 1179656 | tf_op jit(solution)/shard_map/ppermute | solution.py:24
  46.5 16.6 %collective-permute-start.8 = (f32[128,256]{1,0:T(8,128)S(1)}, f32[128,256]{1,0:T(8,128)S(1)}, u32[]{:S(2)}, u32[]{:S(2)}) collective-permute-start(f32[128,256]{1,0:T(8,128)S(1)} %collective-permute-done.7), channel_id=1, source_target_pairs={{241,255},{78,64},{49,63},{142,128},{113,127},{206,192},{177,191},... | collective-permute-start | bytes 393224 | tf_op jit(solution)/shard_map/ppermute | solution.py:176
  47.8 15.3 %collective-permute-start.6 = (f32[128,256]{1,0:T(8,128)S(1)}, f32[128,256]{1,0:T(8,128)S(1)}, u32[]{:S(2)}, u32[]{:S(2)}) collective-permute-start(f32[128,256]{1,0:T(8,128)S(1)} %slice.33), channel_id=1, source_target_pairs={{1,2},{2,1},{3,4},{4,3},{5,6},{6,5},{7,8},{8,7},{9,10},{10,9},{11,... | collective-permute-start | bytes 393224 | tf_op jit(solution)/shard_map/ppermute | solution.py:168

commit v4 on v3

--- a/solution.py
+++ b/solution.py
@@ -67,19 +67,27 @@
     )(tile_pattern, integrals)
 
 
+def product(vh_ref, vl_ref, t_ref):
+    th, tl = split(t_ref[...])
+    vh, vl = vh_ref[0], vl_ref[0]
+    dot = functools.partial(jnp.dot, preferred_element_type=jnp.float32)
+    return dot(vh, th) + (dot(vh, tl) + dot(vl, th))
+
+
 def add_kernel(count, *refs):
     *blocks, acc_ref, out_ref = refs
     total = acc_ref[...]
     for i in range(count):
-        vh_ref, vl_ref, t_ref = blocks[3 * i : 3 * i + 3]
-        th, tl = split(t_ref[...])
-        vh, vl = vh_ref[0], vl_ref[0]
-        dot = functools.partial(jnp.dot, preferred_element_type=jnp.float32)
-        total += dot(vh, th) + (dot(vh, tl) + dot(vl, th))
+        total += product(*blocks[3 * i : 3 * i + 3])
     out_ref[...] = total
-
-
-def add_products(acc, high, low, parts, cols, name):
+    if len(blocks) > 3 * count:
+
+        @pl.when(pl.program_id(0) == pl.num_programs(0) - 1)
+        def _():
+            out_ref[...] += product(*blocks[3 * count :])
+
+
+def add_products(acc, high, low, parts, cols, name, flops, edge=()):
     rows, width = acc.shape
     args, specs = [], []
     for role, piece, block in parts:
@@ -87,6 +95,11 @@
         spec = pl.BlockSpec((1, rows, deep), lambda j, role=role, piece=piece: (role, 0, piece))
         args += [high, low, block]
         specs += [spec, spec, pl.BlockSpec((deep, cols), lambda j: (0, j))]
+    for role, piece, block in edge:
+        deep = block.shape[0]
+        spec = pl.BlockSpec((1, rows, deep), lambda j, role=role, piece=piece: (role, 0, piece))
+        args += [high, low, block]
+        specs += [spec, spec, pl.BlockSpec((deep, cols), lambda j: (0, 0))]
     args.append(acc)
     specs.append(pl.BlockSpec((rows, cols), lambda j: (0, j)))
     n = len(parts)
@@ -97,7 +110,7 @@
         out_specs=pl.BlockSpec((rows, cols), lambda j: (0, j)),
         out_shape=jax.ShapeDtypeStruct(acc.shape, acc.dtype),
         compiler_params=pltpu.CompilerParams(vmem_limit_bytes=32 * 2**20),
-        cost_estimate=pl.CostEstimate(flops=1, bytes_accessed=1, transcendentals=0),
+        cost_estimate=pl.CostEstimate(flops=flops, bytes_accessed=1, transcendentals=0),
         name=name,
     )(*args)
 
@@ -110,10 +123,7 @@
     for i in range(stage.shape[1] // step):
         here = slice(i * step, i * step + step)
         there = slice(start + i * step, start + i * step + step)
-        block = [ref[:, here] for ref in block_refs]
-        if count == 3:
-            block = [jnp.concatenate([block[0], block[1] + block[2]], 0)]
-        th, tl = split(block[0])
+        th, tl = split(jnp.concatenate([ref[:, here] for ref in block_refs], 0))
         vh, vl = high_ref[BEYOND], low_ref[BEYOND]
         dot = functools.partial(jnp.dot, preferred_element_type=jnp.float32)
         stage[:, here] = acc_ref[:, there] + (dot(vh, th) + (dot(vh, tl) + dot(vl, th)))
@@ -146,42 +156,43 @@
     )(*args)
 
 
-def hops(count):
-    facing = [(i, (i + 1 if i % 2 else i - 1) % count) for i in range(count)]
-    far = [pair for pair in facing if {i // 64 for i in pair} != {pair[0] // 64}]
-    return facing, far
+def around(value):
+    count = lax.axis_size(AXIS)
+    routes = []
+    for b in range(0, count, 16):
+        routes.append([i % count for i in (b - 1, b + 9, b + 3, b)])
+        routes.append([i % count for i in (b, b - 10, b - 4, b - 1)])
+    for hop in range(3):
+        value = lax.ppermute(value, AXIS, [(route[hop], route[hop + 1]) for route in routes])
+    return value
+
+
+def inside(value):
+    count = lax.axis_size(AXIS)
+    pairs = [(i, i + 1 if i % 2 else i - 1) for i in range(count) if i % 16 not in (0, 15)]
+    return lax.ppermute(value, AXIS, pairs)
 
 
 def per_device(integrals, tile_pattern, amplitudes, residual_in):
     rows, width = amplitudes.shape
-    count = lax.axis_size(AXIS)
-    pairs, far = hops(count)
-    near = [pair for pair in pairs if pair not in far]
-    cut, kept = 1024, rows - 128
+    cut, kept = 1024, rows - 208
     facing = exchange(amplitudes, 1)
     high, low = align(integrals, tile_pattern)
     n = rows // 2
     pieces = [exchange(amplitudes[i : i + n], 0) for i in range(0, rows, n)]
     partner = jnp.concatenate(pieces, 0)
     most = exchange(partner[:, :cut], 1)
-    rest = exchange(partner[:kept, cut:], 1)
-    slab = lax.ppermute(partner[kept:, cut:], AXIS, near)
-    out, back = [], []
-    for source, target in far:
-        holder = source ^ 1
-        relay = (holder + 16 if source % 2 else holder - 16) % count
-        out.append((holder, relay))
-        back.append((relay, target))
-    held = lax.ppermute(amplitudes[kept:, cut:], AXIS, out)
-    relayed = lax.ppermute(held, AXIS, back)
-    acc = add_products(residual_in, high, low, [(OWN, 0, amplitudes), (PARTNER, 0, partner)], 256, "near")
-    facing, acc = lax.optimization_barrier((facing, acc))
+    rest = [exchange(partner[:kept, cut:], 1), inside(partner[kept:, cut:])]
+    moved = around(partner[kept:, cut:])
+    moved = jnp.pad(moved, ((48, 0), (0, 0)))
+    acc = add_products(residual_in, high, low, [(OWN, 0, amplitudes), (PARTNER, 0, partner)], 256, "near", 12 * rows * rows * width)
+    facing, acc, moved = lax.optimization_barrier((facing, acc, moved))
     n = rows // 2
     beside = [exchange(facing[i : i + n], 0) for i in range(0, rows, n)]
     parts = [(FACING, 0, facing), (BESIDE, 0, jnp.concatenate(beside, 0))]
-    acc = add_products(acc, high, low, parts, 256, "middle")
+    acc = add_products(acc, high, low, parts, 256, "middle", 1, [(BEYOND, 1, moved)])
     result = add_last(acc, high, low, [most], 0, None, "last0")
-    return add_last(acc, high, low, [rest, slab, relayed], cut, result, "last1")
+    return add_last(acc, high, low, rest, cut, result, "last1")
 
 
 def solution(mesh):

time: 66 us -> 65.1 us (0.986)
  waiting for transfers between devices: 23.8 us -> 17.9 us
  starting transfers between devices: 20.3 us -> 25.4 us
    ppermute x7, waiting for transfers between devices: 23.8 us -> 3.77 us  [exchange(): return lax.ppermute(value, AXIS, pairs)]
    ppermute x3 -> x4, waiting for transfers between devices: 0.01 us -> 14.2 us  [the longest x3 14.2 us: around(): lax.ppermute(value, AXIS, [(route[hop], route[hop + 1]) for route in rout...]
    ppermute x3 -> x4, starting transfers between devices: 2.62 us -> 6.99 us  [the longest x3 6.33 us: around(): lax.ppermute(value, AXIS, [(route[hop], route[hop + 1]) for route in rout...]
    ppermute x7, starting transfers between devices: 17.7 us -> 18.4 us  [exchange(): return lax.ppermute(value, AXIS, pairs)]
  transfers between devices with their start and end apart: 10 -> 11, of which waited for: 5 -> 5; matrix products, arithmetic and copies ran while one was open for 4% -> 4% of each run, Pallas kernels for 25% -> 26%
where the time goes in v4:
time: 65.1 us; the launch traced here: 64.9 us
  starting transfers between devices  25.4 us (39%)
  Pallas kernels  18.2 us (28%)
  waiting for transfers between devices  17.9 us (27%)
  local copies, waits for them, and re-layouts  3.05 us (5%)
    ppermute x7, starting transfers between devices, exchange(): return lax.ppermute(value, AXIS, pairs)  18.4 us
    ppermute x3, waiting for transfers between devices, around(): lax.ppermute(value, AXIS, [(route[hop], route[hop + 1]) for route in rout...  14.2 us
    pallas_call x2, Pallas kernels, add_products(): pl.pallas_call(functools.partial(add_kernel, n), grid=(width // cols,), i...  11.8 us
    ppermute x3, starting transfers between devices, around(): lax.ppermute(value, AXIS, [(route[hop], route[hop + 1]) for route in rout...  6.33 us
    pallas_call x2, Pallas kernels, add_last(): pl.pallas_call(functools.partial(last_kernel, start, step, len(blocks)),...  4.28 us
    ppermute x7, waiting for transfers between devices, exchange(): return lax.ppermute(value, AXIS, pairs)  3.77 us
    pallas_call x1, Pallas kernels, align(): pl.pallas_call(functools.partial(align_kernel, tiles), grid=(tiles,), in_...  2.08 us
    slice x1, local copies, waits for them, and re-layouts, per_device(): pieces = [exchange(amplitudes[i:i + n], 0) for i in range(0, rows, n)]  1.88 us
  transfers between devices with their start and end apart: 11, of which 5 were waited for; matrix products, arithmetic and copies ran while one was open for 4% of the time, Pallas kernels for 26%

profile of v4, /device:TPU:0, one launch (start us, length us, event | category | flops | bytes accessed | tf_op | source)
XLA Modules:
  0.0 64.9 jit_solution(8399126249501197519)
XLA Ops:
  0.0 0.0 copy-start.3
  0.0 0.0 copy-start.1
  0.0 8.2 %collective-permute-start = (f32[512,1280]{1,0:T(8,128)}, f32[512,1280]{1,0:T(8,128)S(1)}, u32[]{:S(2)}, u32[]{:S(2)}) collective-permute-start(f32[512,1280]{1,0:T(8,128)} %refs_2_.1), channel_id=1, source_target_pairs={{1,2},{2,1},{3,4},{4,3},{5,6},{6,5},{7,8},{8,7},{9,10},{10,9},{11,... | collective-permute-start | bytes 7864328 | tf_op jit(solution)/shard_map/ppermute | solution.py:24
  8.2 1.9 %fusion.1 = (f32[256,1280]{1,0:T(8,128)S(1)}, f32[256,1280]{1,0:T(8,128)S(1)}) fusion(f32[512,1280]{1,0:T(8,128)} %refs_2_.1), kind=kLoop, calls=%fused_computation.4 | loop fusion | bytes 5242880 | tf_op jit(solution)/shard_map/slice | solution.py:182
  10.1 0.1 collective-permute-start.2
  10.2 0.5 collective-permute-start.1
  10.7 0.0 copy-done.3
  10.7 0.0 copy-done.1
  10.7 2.1 %align.1 = (bf16[5,512,512]{2,1,0:T(8,128)(2,1)S(1)}, bf16[5,512,512]{2,1,0:T(8,128)(2,1)S(1)}) custom-call(s32[4,17]{1,0:T(4,128)S(1)} %copy-done.3, f32[512,2176]{1,0:T(8,128)S(1)} %copy-done.1), custom_call_target="tpu_custom_call" | custom-call | flops 2621440 | bytes 10000000 | tf_op jit(solution)/shard_map/align/pallas_call | solution.py:55
  12.8 0.4 collective-permute-done.2
  13.2 4.1 %collective-permute-start.3 = (f32[208,256]{1,0:T(8,128)S(1)}, f32[208,256]{1,0:T(8,128)S(1)}, u32[]{:S(2)}, u32[]{:S(2)}) collective-permute-start(f32[208,256]{1,0:T(8,128)S(1)} %slice.29), channel_id=1, source_target_pairs={{255,9},{0,246},{15,25},{16,6},{31,41},{32,22},{47,57},{48,38},{63... | collective-permute-start | bytes 638984 | tf_op jit(solution)/shard_map/ppermute | solution.py:166
  17.4 0.0 collective-permute-done.1
  17.4 0.1 constant_dynamic-update-slice_fusion.1
  17.5 5.6 %collective-permute-done.3 = f32[208,256]{1,0:T(8,128)S(1)} collective-permute-done((f32[208,256]{1,0:T(8,128)S(1)}, f32[208,256]{1,0:T(8,128)S(1)}, u32[]{:S(2)}, u32[]{:S(2)}) %collective-permute-start.3) | collective-permute-done | bytes 213024 | tf_op jit(solution)/shard_map/ppermute | solution.py:166
  23.0 0.7 %collective-permute-start.4 = (f32[208,256]{1,0:T(8,128)S(1)}, f32[208,256]{1,0:T(8,128)S(1)}, u32[]{:S(2)}, u32[]{:S(2)}) collective-permute-start(f32[208,256]{1,0:T(8,128)S(1)} %collective-permute-done.3), channel_id=1, source_target_pairs={{9,3},{246,252},{25,19},{6,12},{41,35},{22,28},{57,51},{38,44},{73... | collective-permute-start | bytes 638984 | tf_op jit(solution)/shard_map/ppermute | solution.py:166
  23.7 0.0 copy-start.2
  23.7 0.1 constant_dynamic-update-slice_fusion.refs_5_
  23.8 0.0 copy-start
  23.8 0.3 slice.31
  24.1 0.1 collective-permute-start.10
  24.2 0.0 collective-permute-done.4
  24.2 1.6 %collective-permute-start.5 = (f32[208,256]{1,0:T(8,128)S(1)}, f32[208,256]{1,0:T(8,128)S(1)}, u32[]{:S(2)}, u32[]{:S(2)}) collective-permute-start(f32[208,256]{1,0:T(8,128)S(1)} %collective-permute-done.4), channel_id=1, source_target_pairs={{3,0},{252,255},{19,16},{12,15},{35,32},{28,31},{51,48},{44,47},{6... | collective-permute-start | bytes 638984 | tf_op jit(solution)/shard_map/ppermute | solution.py:166
  25.8 0.0 copy-done.2
  25.8 0.5 copy-done
  26.3 5.6 %near.1.refs_9_ = f32[512,1280]{1,0:T(8,128)S(1)} custom-call(bf16[5,512,512]{2,1,0:T(8,128)(2,1)S(1)} %get-tuple-element.10.refs_0_.refs_3_.refs_6_, bf16[5,512,512]{2,1,0:T(8,128)(2,1)S(1)} %get-tuple-element.11.refs_1_.refs_4_.refs_7_, f32[512,1280]{1,0:T(8,128)S(1)} %copy-done, bf16[5,512,512]{2,1,0:T(8,128)(2,1)S(1)} %get-tuple-element.10.refs_0_.refs_3_.refs_6_, ...), custom_call_target="tpu_custom_call" | custom-call | flops 4026531840 | bytes 1 | tf_op jit(solution)/shard_map/near/pallas_call | solution.py:106
  31.9 8.6 %collective-permute-done.5 = f32[208,256]{1,0:T(8,128)S(1)} collective-permute-done((f32[208,256]{1,0:T(8,128)S(1)}, f32[208,256]{1,0:T(8,128)S(1)}, u32[]{:S(2)}, u32[]{:S(2)}) %collective-permute-start.5) | collective-permute-done | bytes 213024 | tf_op jit(solution)/shard_map/ppermute | solution.py:166
  40.5 0.0 collective-permute-done.refs_2_
  40.5 0.2 fusion
  40.7 0.1 collective-permute-start.6
  40.8 0.5 collective-permute-start.7
  41.3 0.7 %collective-permute-start.9 = (f32[208,256]{1,0:T(8,128)S(1)}, f32[208,256]{1,0:T(8,128)S(1)}, u32[]{:S(2)}, u32[]{:S(2)}) collective-permute-start(f32[208,256]{1,0:T(8,128)S(1)} %slice.29), channel_id=1, source_target_pairs={{1,2},{2,1},{3,4},{4,3},{5,6},{6,5},{7,8},{8,7},{9,10},{10,9},{11,... | collective-permute-start | bytes 638984 | tf_op jit(solution)/shard_map/ppermute | solution.py:173
  42.0 9.0 %collective-permute-start.8 = (f32[304,256]{1,0:T(8,128)S(1)}, f32[304,256]{1,0:T(8,128)S(1)}, u32[]{:S(2)}, u32[]{:S(2)}) collective-permute-start(f32[304,256]{1,0:T(8,128)S(1)} %slice.30), channel_id=1, source_target_pairs={{1,2},{2,1},{3,4},{4,3},{5,6},{6,5},{7,8},{8,7},{9,10},{10,9},{11,... | collective-permute-start | bytes 933896 | tf_op jit(solution)/shard_map/ppermute | solution.py:24
  51.0 0.0 collective-permute-done.6
  51.0 0.0 collective-permute-done.7
  51.0 0.2 pad_maximum_fusion.refs_5_
  51.1 6.2 %middle.1.refs_2_ = f32[512,1280]{1,0:T(8,128)S(1)} custom-call(bf16[5,512,512]{2,1,0:T(8,128)(2,1)S(1)} %get-tuple-element.10.refs_0_.refs_3_.refs_6_, bf16[5,512,512]{2,1,0:T(8,128)(2,1)S(1)} %get-tuple-element.11.refs_1_.refs_4_.refs_7_, f32[512,1280]{1,0:T(8,128)S(1)} %collective-permute-done.refs_2_, ...), custom_call_target="tpu_custom_call" | custom-call | flops 1 | bytes 1 | tf_op jit(solution)/shard_map/middle/pallas_call | solution.py:106
  57.3 2.9 %collective-permute-done.10.refs_3_ = f32[512,1024]{1,0:T(8,128)S(1)} collective-permute-done((f32[512,1024]{1,0:T(8,128)S(1)}, f32[512,1024]{1,0:T(8,128)S(1)}, u32[]{:S(2)}, u32[]{:S(2)}) %collective-permute-start.10) | collective-permute-done | bytes 2097184 | tf_op jit(solution)/shard_map/ppermute | solution.py:24
  60.2 2.9 %last0.1.refs_5_ = f32[512,1280]{1,0:T(8,128)} custom-call(bf16[5,512,512]{2,1,0:T(8,128)(2,1)S(1)} %get-tuple-element.10.refs_0_.refs_3_.refs_6_, bf16[5,512,512]{2,1,0:T(8,128)(2,1)S(1)} %get-tuple-element.11.refs_1_.refs_4_.refs_7_, f32[512,1280]{1,0:T(8,128)S(1)} %middle.1.refs_2_, f32[512,1024]{1,0:T(8,128)S(1)} %collective-permute-done.10.refs_3_), custom_call_target="tpu_custom_call" | custom-call | flops 1 | bytes 1 | tf_op jit(solution)/shard_map/last0/pallas_call | solution.py:146
  63.1 0.0 collective-permute-done.9.refs_4_
  63.1 0.4 collective-permute-done.8.refs_3_
  63.6 1.4 %last1.1 = f32[512,1280]{1,0:T(8,128)} custom-call(bf16[5,512,512]{2,1,0:T(8,128)(2,1)S(1)} %get-tuple-element.10.refs_0_.refs_3_.refs_6_, bf16[5,512,512]{2,1,0:T(8,128)(2,1)S(1)} %get-tuple-element.11.refs_1_.refs_4_.refs_7_, f32[512,1280]{1,0:T(8,128)S(1)} %middle.1.refs_2_, ...), custom_call_target="tpu_custom_call", output_to_operand_aliasing={{}: (5, {})} | custom-call | flops 1 | bytes 1 | tf_op jit(solution)/shard_map/last1/pallas_call | solution.py:146
  (3 shorter events, 0.1 us)
Async XLA Ops:
  0.0 10.7 %copy-start.3 = (s32[4,17]{1,0:T(4,128)S(1)}, s32[4,17]{1,0:T(4,128)}, u32[]{:S(2)}) copy-start(s32[4,17]{1,0:T(4,128)} %pattern_ref.1) | copy-start | bytes 820
  0.0 10.7 %copy-start.1 = (f32[512,2176]{1,0:T(8,128)S(1)}, f32[512,2176]{1,0:T(8,128)}, u32[]{:S(2)}) copy-start(f32[512,2176]{1,0:T(8,128)} %v_ref.1) | copy-start | bytes 13369348
  0.0 40.5 %collective-permute-start = (f32[512,1280]{1,0:T(8,128)}, f32[512,1280]{1,0:T(8,128)S(1)}, u32[]{:S(2)}, u32[]{:S(2)}) collective-permute-start(f32[512,1280]{1,0:T(8,128)} %refs_2_.1), channel_id=1, source_target_pairs={{1,2},{2,1},{3,4},{4,3},{5,6},{6,5},{7,8},{8,7},{9,10},{10,9},{11,... | collective-permute-start | bytes 7864328 | tf_op jit(solution)/shard_map/ppermute | solution.py:24
  10.1 3.1 %collective-permute-start.2 = (f32[256,1280]{1,0:T(8,128)S(1)}, f32[256,1280]{1,0:T(8,128)S(1)}, u32[]{:S(2)}, u32[]{:S(2)}) collective-permute-start(f32[256,1280]{1,0:T(8,128)S(1)} %get-tuple-element.17), channel_id=1, source_target_pairs={{0,1},{1,0},{2,3},{3,2},{4,5},{5,4},{6,7},{7,6},{8,9},{9,8},{10,11... | collective-permute-start | bytes 3932168 | tf_op jit(solution)/shard_map/ppermute | solution.py:24
  10.2 7.2 %collective-permute-start.1 = (f32[256,1280]{1,0:T(8,128)S(1)}, f32[256,1280]{1,0:T(8,128)S(1)}, u32[]{:S(2)}, u32[]{:S(2)}) collective-permute-start(f32[256,1280]{1,0:T(8,128)S(1)} %get-tuple-element.18), channel_id=1, source_target_pairs={{0,1},{1,0},{2,3},{3,2},{4,5},{5,4},{6,7},{7,6},{8,9},{9,8},{10,11... | collective-permute-start | bytes 3932168 | tf_op jit(solution)/shard_map/ppermute | solution.py:24
  13.2 9.8 %collective-permute-start.3 = (f32[208,256]{1,0:T(8,128)S(1)}, f32[208,256]{1,0:T(8,128)S(1)}, u32[]{:S(2)}, u32[]{:S(2)}) collective-permute-start(f32[208,256]{1,0:T(8,128)S(1)} %slice.29), channel_id=1, source_target_pairs={{255,9},{0,246},{15,25},{16,6},{31,41},{32,22},{47,57},{48,38},{63... | collective-permute-start | bytes 638984 | tf_op jit(solution)/shard_map/ppermute | solution.py:166
  23.0 1.2 %collective-permute-start.4 = (f32[208,256]{1,0:T(8,128)S(1)}, f32[208,256]{1,0:T(8,128)S(1)}, u32[]{:S(2)}, u32[]{:S(2)}) collective-permute-start(f32[208,256]{1,0:T(8,128)S(1)} %collective-permute-done.3), channel_id=1, source_target_pairs={{9,3},{246,252},{25,19},{6,12},{41,35},{22,28},{57,51},{38,44},{73... | collective-permute-start | bytes 638984 | tf_op jit(solution)/shard_map/ppermute | solution.py:166
  23.7 2.1 %copy-start.2 = (f32[512,1280]{1,0:T(8,128)S(1)}, f32[512,1280]{1,0:T(8,128)}, u32[]{:S(2)}) copy-start(f32[512,1280]{1,0:T(8,128)} %refs_6_.1) | copy-start | bytes 7864324
  23.8 2.5 %copy-start = (f32[512,1280]{1,0:T(8,128)S(1)}, f32[512,1280]{1,0:T(8,128)}, u32[]{:S(2)}) copy-start(f32[512,1280]{1,0:T(8,128)} %refs_2_.1) | copy-start | bytes 7864324
  24.1 36.1 %collective-permute-start.10 = (f32[512,1024]{1,0:T(8,128)S(1)}, f32[512,1024]{1,0:T(8,128)S(1)}, u32[]{:S(2)}, u32[]{:S(2)}) collective-permute-start(f32[512,1024]{1,0:T(8,128)S(1)} %slice.31), channel_id=1, source_target_pairs={{1,2},{2,1},{3,4},{4,3},{5,6},{6,5},{7,8},{8,7},{9,10},{10,9},{11,... | collective-permute-start | bytes 6291464 | tf_op jit(solution)/shard_map/ppermute | solution.py:24
  24.2 16.3 %collective-permute-start.5 = (f32[208,256]{1,0:T(8,128)S(1)}, f32[208,256]{1,0:T(8,128)S(1)}, u32[]{:S(2)}, u32[]{:S(2)}) collective-permute-start(f32[208,256]{1,0:T(8,128)S(1)} %collective-permute-done.4), channel_id=1, source_target_pairs={{3,0},{252,255},{19,16},{12,15},{35,32},{28,31},{51,48},{44,47},{6... | collective-permute-start | bytes 638984 | tf_op jit(solution)/shard_map/ppermute | solution.py:166
  40.7 10.3 %collective-permute-start.6 = (f32[256,1280]{1,0:T(8,128)S(1)}, f32[256,1280]{1,0:T(8,128)S(1)}, u32[]{:S(2)}, u32[]{:S(2)}) collective-permute-start(f32[256,1280]{1,0:T(8,128)S(1)} %get-tuple-element.15), channel_id=1, source_target_pairs={{0,1},{1,0},{2,3},{3,2},{4,5},{5,4},{6,7},{7,6},{8,9},{9,8},{10,11... | collective-permute-start | bytes 3932168 | tf_op jit(solution)/shard_map/ppermute | solution.py:24
  40.8 10.2 %collective-permute-start.7 = (f32[256,1280]{1,0:T(8,128)S(1)}, f32[256,1280]{1,0:T(8,128)S(1)}, u32[]{:S(2)}, u32[]{:S(2)}) collective-permute-start(f32[256,1280]{1,0:T(8,128)S(1)} %get-tuple-element.16), channel_id=1, source_target_pairs={{0,1},{1,0},{2,3},{3,2},{4,5},{5,4},{6,7},{7,6},{8,9},{9,8},{10,11... | collective-permute-start | bytes 3932168 | tf_op jit(solution)/shard_map/ppermute | solution.py:24
  41.3 21.8 %collective-permute-start.9 = (f32[208,256]{1,0:T(8,128)S(1)}, f32[208,256]{1,0:T(8,128)S(1)}, u32[]{:S(2)}, u32[]{:S(2)}) collective-permute-start(f32[208,256]{1,0:T(8,128)S(1)} %slice.29), channel_id=1, source_target_pairs={{1,2},{2,1},{3,4},{4,3},{5,6},{6,5},{7,8},{8,7},{9,10},{10,9},{11,... | collective-permute-start | bytes 638984 | tf_op jit(solution)/shard_map/ppermute | solution.py:173
  42.0 21.6 %collective-permute-start.8 = (f32[304,256]{1,0:T(8,128)S(1)}, f32[304,256]{1,0:T(8,128)S(1)}, u32[]{:S(2)}, u32[]{:S(2)}) collective-permute-start(f32[304,256]{1,0:T(8,128)S(1)} %slice.30), channel_id=1, source_target_pairs={{1,2},{2,1},{3,4},{4,3},{5,6},{6,5},{7,8},{8,7},{9,10},{10,9},{11,... | collective-permute-start | bytes 933896 | tf_op jit(solution)/shard_map/ppermute | solution.py:24

commit v5 on v4

--- a/solution.py
+++ b/solution.py
@@ -115,6 +115,14 @@
     )(*args)
 
 
+def joined(pieces):
+    if len(pieces) == 1:
+        return pieces[0]
+    rest, inner, short = pieces
+    cut = short.shape[0]
+    return jnp.concatenate([rest, inner[:cut] + short, inner[cut:]], 0)
+
+
 def last_kernel(start, step, count, *refs):
     high_ref, low_ref, acc_ref = refs[:3]
     block_refs = refs[3 : 3 + count]
@@ -123,7 +131,7 @@
     for i in range(stage.shape[1] // step):
         here = slice(i * step, i * step + step)
         there = slice(start + i * step, start + i * step + step)
-        th, tl = split(jnp.concatenate([ref[:, here] for ref in block_refs], 0))
+        th, tl = split(joined([ref[:, here] for ref in block_refs]))
         vh, vl = high_ref[BEYOND], low_ref[BEYOND]
         dot = functools.partial(jnp.dot, preferred_element_type=jnp.float32)
         stage[:, here] = acc_ref[:, there] + (dot(vh, th) + (dot(vh, tl) + dot(vl, th)))
@@ -156,36 +164,49 @@
     )(*args)
 
 
-def around(value):
+def facing_pairs(kind):
     count = lax.axis_size(AXIS)
-    routes = []
+    pairs = [(i, (i + 1 if i % 2 else i - 1) % count) for i in range(count)]
+    ends = {"inside": (1, 16), "x": (16, 64), "y": (64, count + 1)}[kind]
+    border = lambda i: next(size for size in (count, 64, 16, 1) if size <= count and (i + 1) % size < 2)
+    return [pair for pair in pairs if ends[0] <= border(pair[0]) < ends[1]]
+
+
+def detours(one, two):
+    count = lax.axis_size(AXIS)
+    along, beside = [[], [], []], [[], []]
     for b in range(0, count, 16):
-        routes.append([i % count for i in (b - 1, b + 9, b + 3, b)])
-        routes.append([i % count for i in (b, b - 10, b - 4, b - 1)])
-    for hop in range(3):
-        value = lax.ppermute(value, AXIS, [(route[hop], route[hop + 1]) for route in routes])
-    return value
-
-
-def inside(value):
-    count = lax.axis_size(AXIS)
-    pairs = [(i, i + 1 if i % 2 else i - 1) for i in range(count) if i % 16 not in (0, 15)]
-    return lax.ppermute(value, AXIS, pairs)
+        for route in ((b - 1, b + 9, b + 3, b), (b, b - 10, b - 4, b - 1)):
+            for hop, (i, j) in enumerate(zip(route, route[1:])):
+                along[hop].append((i % count, j % count))
+    for b in range(0, count, 64):
+        for route in ((b - 2, b + 14, b), (b + 1, b - 15, b - 1)):
+            for hop, (i, j) in enumerate(zip(route, route[1:])):
+                beside[hop].append((i % count, j % count))
+    for pairs in along:
+        one = lax.ppermute(one, AXIS, pairs)
+    for pairs in beside:
+        two = lax.ppermute(two, AXIS, pairs)
+    return one, two
 
 
 def per_device(integrals, tile_pattern, amplitudes, residual_in):
     rows, width = amplitudes.shape
-    cut, kept = 1024, rows - 208
+    deep = 128
+    cut, first, second = 1024, rows - 2 * deep, rows - deep
     facing = exchange(amplitudes, 1)
     high, low = align(integrals, tile_pattern)
     n = rows // 2
     pieces = [exchange(amplitudes[i : i + n], 0) for i in range(0, rows, n)]
     partner = jnp.concatenate(pieces, 0)
     most = exchange(partner[:, :cut], 1)
-    rest = [exchange(partner[:kept, cut:], 1), inside(partner[kept:, cut:])]
-    moved = around(partner[kept:, cut:])
-    moved = jnp.pad(moved, ((48, 0), (0, 0)))
-    acc = add_products(residual_in, high, low, [(OWN, 0, amplitudes), (PARTNER, 0, partner)], 256, "near", 12 * rows * rows * width)
+    rest = [exchange(partner[:first, cut:], 1)]
+    rest.append(lax.ppermute(partner[first:, cut:], AXIS, facing_pairs("inside")))
+    rest.append(lax.ppermute(partner[first:second, cut:], AXIS, facing_pairs("x")))
+    mine, partner = lax.optimization_barrier((amplitudes, partner))
+    one, two = detours(partner[second:, cut:], mine[first:second, cut:])
+    moved = jnp.concatenate([two, one], 0)
+    acc = add_products(residual_in, high, low, [(OWN, 0, amplitudes), (PARTNER, 0, partner)], 256, "near", 6 * rows * rows * width)
     facing, acc, moved = lax.optimization_barrier((facing, acc, moved))
     n = rows // 2
     beside = [exchange(facing[i : i + n], 0) for i in range(0, rows, n)]

time: 65.1 us -> 64.7 us (level)
  waiting for transfers between devices: 17.9 us -> 15.6 us
  starting transfers between devices: 25.4 us -> 27.5 us
    ppermute x4 -> x7, waiting for transfers between devices: 14.2 us -> 5.49 us  [the longest x3 4.23 us: detours(): one = lax.ppermute(one, AXIS, pairs)]
    ppermute x7, waiting for transfers between devices: 3.77 us -> 10.2 us  [exchange(): return lax.ppermute(value, AXIS, pairs)]
    ppermute x4 -> x7, starting transfers between devices: 6.99 us -> 9.5 us  [the longest x3 6.06 us: detours(): one = lax.ppermute(one, AXIS, pairs)]
  transfers between devices with their start and end apart: 11 -> 14, of which waited for: 5 -> 8; matrix products, arithmetic and copies ran while one was open for 4% -> 5% of each run, Pallas kernels for 26% -> 26%
where the time goes in v5:
time: 64.7 us; the launch traced here: 64.5 us
  starting transfers between devices  27.5 us (43%)
  Pallas kernels  18.2 us (28%)
  waiting for transfers between devices  15.6 us (24%)
  local copies, waits for them, and re-layouts  2.75 us (4%)
    ppermute x7, starting transfers between devices, exchange(): return lax.ppermute(value, AXIS, pairs)  18 us
    pallas_call x2, Pallas kernels, add_products(): pl.pallas_call(functools.partial(add_kernel, n), grid=(width // cols,), i...  11.8 us
    ppermute x7, waiting for transfers between devices, exchange(): return lax.ppermute(value, AXIS, pairs)  10.2 us
    ppermute x3, starting transfers between devices, detours(): one = lax.ppermute(one, AXIS, pairs)  6.06 us
    pallas_call x2, Pallas kernels, add_last(): pl.pallas_call(functools.partial(last_kernel, start, step, len(blocks)),...  4.29 us
    ppermute x3, waiting for transfers between devices, detours(): one = lax.ppermute(one, AXIS, pairs)  4.23 us
    pallas_call x1, Pallas kernels, align(): pl.pallas_call(functools.partial(align_kernel, tiles), grid=(tiles,), in_...  2.1 us
    ppermute x2, starting transfers between devices, detours(): two = lax.ppermute(two, AXIS, pairs)  2.09 us
  transfers between devices with their start and end apart: 14, of which 8 were waited for; matrix products, arithmetic and copies ran while one was open for 5% of the time, Pallas kernels for 26%

profile of v5, /device:TPU:0, one launch (start us, length us, event | category | flops | bytes accessed | tf_op | source)
XLA Modules:
  0.0 64.5 jit_solution(851685515875531729)
XLA Ops:
  0.0 8.2 %collective-permute-start = (f32[512,1280]{1,0:T(8,128)}, f32[512,1280]{1,0:T(8,128)S(1)}, u32[]{:S(2)}, u32[]{:S(2)}) collective-permute-start(f32[512,1280]{1,0:T(8,128)} %refs_2_.1), channel_id=1, source_target_pairs={{1,2},{2,1},{3,4},{4,3},{5,6},{6,5},{7,8},{8,7},{9,10},{10,9},{11,... | collective-permute-start | bytes 7864328 | tf_op jit(solution)/shard_map/ppermute | solution.py:24
  8.2 0.0 copy-start.1
  8.2 2.0 %fusion.1 = (f32[256,1280]{1,0:T(8,128)S(1)}, f32[256,1280]{1,0:T(8,128)S(1)}) fusion(f32[512,1280]{1,0:T(8,128)} %refs_2_.1), kind=kLoop, calls=%fused_computation.5 | loop fusion | bytes 5242880 | tf_op jit(solution)/shard_map/slice | solution.py:200
  10.2 0.1 collective-permute-start.1
  10.3 0.0 copy-start
  10.4 0.0 copy-start.3
  10.4 0.5 collective-permute-start.2
  10.8 2.5 %collective-permute-done.1 = f32[256,1280]{1,0:T(8,128)S(1)} collective-permute-done((f32[256,1280]{1,0:T(8,128)S(1)}, f32[256,1280]{1,0:T(8,128)S(1)}, u32[]{:S(2)}, u32[]{:S(2)}) %collective-permute-start.1) | collective-permute-done | bytes 1310752 | tf_op jit(solution)/shard_map/ppermute | solution.py:24
  13.4 0.1 constant_dynamic-update-slice_fusion.1
  13.5 1.8 %collective-permute-done.2 = f32[256,1280]{1,0:T(8,128)S(1)} collective-permute-done((f32[256,1280]{1,0:T(8,128)S(1)}, f32[256,1280]{1,0:T(8,128)S(1)}, u32[]{:S(2)}, u32[]{:S(2)}) %collective-permute-start.2) | collective-permute-done | bytes 1310752 | tf_op jit(solution)/shard_map/ppermute | solution.py:24
  15.2 0.1 constant_dynamic-update-slice_fusion.refs_5_
  15.4 4.1 %collective-permute-start.5 = (f32[128,256]{1,0:T(8,128)S(1)}, f32[128,256]{1,0:T(8,128)S(1)}, u32[]{:S(2)}, u32[]{:S(2)}) collective-permute-start(f32[128,256]{1,0:T(8,128)S(1)} %slice.33), channel_id=1, source_target_pairs={{255,9},{0,246},{15,25},{16,6},{31,41},{32,22},{47,57},{48,38},{63... | collective-permute-start | bytes 393224 | tf_op jit(solution)/shard_map/ppermute | solution.py:187
  19.5 0.0 copy-done
  19.5 0.7 %collective-permute-start.3 = (f32[128,256]{1,0:T(8,128)S(1)}, f32[128,256]{1,0:T(8,128)S(1)}, u32[]{:S(2)}, u32[]{:S(2)}) collective-permute-start(f32[128,256]{1,0:T(8,128)S(1)} %slice.32), channel_id=1, source_target_pairs={{254,14},{1,241},{62,78},{65,49},{126,142},{129,113},{190,206},{19... | collective-permute-start | bytes 393224 | tf_op jit(solution)/shard_map/ppermute | solution.py:189
  20.2 3.2 %collective-permute-done.5 = f32[128,256]{1,0:T(8,128)S(1)} collective-permute-done((f32[128,256]{1,0:T(8,128)S(1)}, f32[128,256]{1,0:T(8,128)S(1)}, u32[]{:S(2)}, u32[]{:S(2)}) %collective-permute-start.5) | collective-permute-done | bytes 131104 | tf_op jit(solution)/shard_map/ppermute | solution.py:187
  23.4 0.7 %collective-permute-start.6 = (f32[128,256]{1,0:T(8,128)S(1)}, f32[128,256]{1,0:T(8,128)S(1)}, u32[]{:S(2)}, u32[]{:S(2)}) collective-permute-start(f32[128,256]{1,0:T(8,128)S(1)} %collective-permute-done.5), channel_id=1, source_target_pairs={{9,3},{246,252},{25,19},{6,12},{41,35},{22,28},{57,51},{38,44},{73... | collective-permute-start | bytes 393224 | tf_op jit(solution)/shard_map/ppermute | solution.py:187
  24.1 0.0 copy-done.1
  24.1 0.0 copy-done.3
  24.1 2.1 %align.1 = (bf16[5,512,512]{2,1,0:T(8,128)(2,1)S(1)}, bf16[5,512,512]{2,1,0:T(8,128)(2,1)S(1)}) custom-call(s32[4,17]{1,0:T(4,128)S(1)} %copy-done.3, f32[512,2176]{1,0:T(8,128)S(1)} %copy-done.1), custom_call_target="tpu_custom_call" | custom-call | flops 2621440 | bytes 10000000 | tf_op jit(solution)/shard_map/align/pallas_call | solution.py:55
  26.2 0.0 copy-start.2
  26.2 0.3 slice.43
  26.5 0.1 collective-permute-start.13
  26.6 0.0 collective-permute-done.3
  26.6 1.4 %collective-permute-start.4 = (f32[128,256]{1,0:T(8,128)S(1)}, f32[128,256]{1,0:T(8,128)S(1)}, u32[]{:S(2)}, u32[]{:S(2)}) collective-permute-start(f32[128,256]{1,0:T(8,128)S(1)} %collective-permute-done.3), channel_id=1, source_target_pairs={{14,0},{241,255},{78,64},{49,63},{142,128},{113,127},{206,192},{17... | collective-permute-start | bytes 393224 | tf_op jit(solution)/shard_map/ppermute | solution.py:189
  28.1 0.0 collective-permute-done.6
  28.1 1.3 %collective-permute-start.7 = (f32[128,256]{1,0:T(8,128)S(1)}, f32[128,256]{1,0:T(8,128)S(1)}, u32[]{:S(2)}, u32[]{:S(2)}) collective-permute-start(f32[128,256]{1,0:T(8,128)S(1)} %collective-permute-done.6), channel_id=1, source_target_pairs={{3,0},{252,255},{19,16},{12,15},{35,32},{28,31},{51,48},{44,47},{6... | collective-permute-start | bytes 393224 | tf_op jit(solution)/shard_map/ppermute | solution.py:187
  29.4 0.0 copy-done.2
  29.4 5.7 %near.1.refs_9_ = f32[512,1280]{1,0:T(8,128)S(1)} custom-call(bf16[5,512,512]{2,1,0:T(8,128)(2,1)S(1)} %get-tuple-element.12.refs_0_.refs_3_.refs_6_, bf16[5,512,512]{2,1,0:T(8,128)(2,1)S(1)} %get-tuple-element.13.refs_1_.refs_4_.refs_7_, f32[512,1280]{1,0:T(8,128)S(1)} %copy-done, bf16[5,512,512]{2,1,0:T(8,128)(2,1)S(1)} %get-tuple-element.12.refs_0_.refs_3_.refs_6_, ...), custom_call_target="tpu_custom_call" | custom-call | flops 2013265920 | bytes 1 | tf_op jit(solution)/shard_map/near/pallas_call | solution.py:106
  35.0 1.3 %collective-permute-done.4 = f32[128,256]{1,0:T(8,128)S(1)} collective-permute-done((f32[128,256]{1,0:T(8,128)S(1)}, f32[128,256]{1,0:T(8,128)S(1)}, u32[]{:S(2)}, u32[]{:S(2)}) %collective-permute-start.4) | collective-permute-done | bytes 131104 | tf_op jit(solution)/shard_map/ppermute | solution.py:189
  36.3 1.0 %collective-permute-done.7 = f32[128,256]{1,0:T(8,128)S(1)} collective-permute-done((f32[128,256]{1,0:T(8,128)S(1)}, f32[128,256]{1,0:T(8,128)S(1)}, u32[]{:S(2)}, u32[]{:S(2)}) %collective-permute-start.7) | collective-permute-done | bytes 131104 | tf_op jit(solution)/shard_map/ppermute | solution.py:187
  37.3 0.4 collective-permute-done.refs_2_
  37.8 0.2 fusion
  37.9 0.1 collective-permute-start.8
  38.0 0.5 collective-permute-start.9
  38.5 0.7 %collective-permute-start.12 = (f32[128,256]{1,0:T(8,128)S(1)}, f32[128,256]{1,0:T(8,128)S(1)}, u32[]{:S(2)}, u32[]{:S(2)}) collective-permute-start(f32[128,256]{1,0:T(8,128)S(1)} %slice.42), channel_id=1, source_target_pairs={{15,16},{16,15},{31,32},{32,31},{47,48},{48,47},{79,80},{80,79},{9... | collective-permute-start | bytes 393224 | tf_op jit(solution)/shard_map/ppermute | solution.py:205
  39.2 0.7 %collective-permute-start.11 = (f32[256,256]{1,0:T(8,128)S(1)}, f32[256,256]{1,0:T(8,128)S(1)}, u32[]{:S(2)}, u32[]{:S(2)}) collective-permute-start(f32[256,256]{1,0:T(8,128)S(1)} %slice.41), channel_id=1, source_target_pairs={{1,2},{2,1},{3,4},{4,3},{5,6},{6,5},{7,8},{8,7},{9,10},{10,9},{11,... | collective-permute-start | bytes 786440 | tf_op jit(solution)/shard_map/ppermute | solution.py:204
  40.0 1.1 %collective-permute-done.8 = f32[256,1280]{1,0:T(8,128)S(1)} collective-permute-done((f32[256,1280]{1,0:T(8,128)S(1)}, f32[256,1280]{1,0:T(8,128)S(1)}, u32[]{:S(2)}, u32[]{:S(2)}) %collective-permute-start.8) | collective-permute-done | bytes 1310752 | tf_op jit(solution)/shard_map/ppermute | solution.py:24
  41.0 8.5 %collective-permute-start.10 = (f32[256,256]{1,0:T(8,128)S(1)}, f32[256,256]{1,0:T(8,128)S(1)}, u32[]{:S(2)}, u32[]{:S(2)}) collective-permute-start(f32[256,256]{1,0:T(8,128)S(1)} %slice.40), channel_id=1, source_target_pairs={{1,2},{2,1},{3,4},{4,3},{5,6},{6,5},{7,8},{8,7},{9,10},{10,9},{11,... | collective-permute-start | bytes 786440 | tf_op jit(solution)/shard_map/ppermute | solution.py:24
  49.6 0.0 collective-permute-done.9
  49.6 0.2 pad_maximum_fusion.refs_5_
  49.7 6.2 %middle.1.refs_2_ = f32[512,1280]{1,0:T(8,128)S(1)} custom-call(bf16[5,512,512]{2,1,0:T(8,128)(2,1)S(1)} %get-tuple-element.12.refs_0_.refs_3_.refs_6_, bf16[5,512,512]{2,1,0:T(8,128)(2,1)S(1)} %get-tuple-element.13.refs_1_.refs_4_.refs_7_, f32[512,1280]{1,0:T(8,128)S(1)} %collective-permute-done.refs_2_, ...), custom_call_target="tpu_custom_call" | custom-call | flops 1 | bytes 1 | tf_op jit(solution)/shard_map/middle/pallas_call | solution.py:106
  55.9 4.3 %collective-permute-done.13.refs_3_ = f32[512,1024]{1,0:T(8,128)S(1)} collective-permute-done((f32[512,1024]{1,0:T(8,128)S(1)}, f32[512,1024]{1,0:T(8,128)S(1)}, u32[]{:S(2)}, u32[]{:S(2)}) %collective-permute-start.13) | collective-permute-done | bytes 2097184 | tf_op jit(solution)/shard_map/ppermute | solution.py:24
  60.2 2.9 %last0.1.refs_6_ = f32[512,1280]{1,0:T(8,128)} custom-call(bf16[5,512,512]{2,1,0:T(8,128)(2,1)S(1)} %get-tuple-element.12.refs_0_.refs_3_.refs_6_, bf16[5,512,512]{2,1,0:T(8,128)(2,1)S(1)} %get-tuple-element.13.refs_1_.refs_4_.refs_7_, f32[512,1280]{1,0:T(8,128)S(1)} %middle.1.refs_2_, f32[512,1024]{1,0:T(8,128)S(1)} %collective-permute-done.13.refs_3_), custom_call_target="tpu_custom_call" | custom-call | flops 1 | bytes 1 | tf_op jit(solution)/shard_map/last0/pallas_call | solution.py:154
  63.1 0.0 collective-permute-done.12.refs_5_
  63.1 0.0 collective-permute-done.11.refs_4_
  63.1 0.0 collective-permute-done.10.refs_3_
  63.2 1.4 %last1.1 = f32[512,1280]{1,0:T(8,128)} custom-call(bf16[5,512,512]{2,1,0:T(8,128)(2,1)S(1)} %get-tuple-element.12.refs_0_.refs_3_.refs_6_, bf16[5,512,512]{2,1,0:T(8,128)(2,1)S(1)} %get-tuple-element.13.refs_1_.refs_4_.refs_7_, f32[512,1280]{1,0:T(8,128)S(1)} %middle.1.refs_2_, ...), custom_call_target="tpu_custom_call", output_to_operand_aliasing={{}: (6, {})} | custom-call | flops 1 | bytes 1 | tf_op jit(solution)/shard_map/last1/pallas_call | solution.py:154
  (6 shorter events, 0.1 us)
Async XLA Ops:
  0.0 37.8 %collective-permute-start = (f32[512,1280]{1,0:T(8,128)}, f32[512,1280]{1,0:T(8,128)S(1)}, u32[]{:S(2)}, u32[]{:S(2)}) collective-permute-start(f32[512,1280]{1,0:T(8,128)} %refs_2_.1), channel_id=1, source_target_pairs={{1,2},{2,1},{3,4},{4,3},{5,6},{6,5},{7,8},{8,7},{9,10},{10,9},{11,... | collective-permute-start | bytes 7864328 | tf_op jit(solution)/shard_map/ppermute | solution.py:24
  8.2 15.9 %copy-start.1 = (f32[512,2176]{1,0:T(8,128)S(1)}, f32[512,2176]{1,0:T(8,128)}, u32[]{:S(2)}) copy-start(f32[512,2176]{1,0:T(8,128)} %v_ref.1) | copy-start | bytes 13369348
  10.2 3.1 %collective-permute-start.1 = (f32[256,1280]{1,0:T(8,128)S(1)}, f32[256,1280]{1,0:T(8,128)S(1)}, u32[]{:S(2)}, u32[]{:S(2)}) collective-permute-start(f32[256,1280]{1,0:T(8,128)S(1)} %get-tuple-element.22), channel_id=1, source_target_pairs={{0,1},{1,0},{2,3},{3,2},{4,5},{5,4},{6,7},{7,6},{8,9},{9,8},{10,11... | collective-permute-start | bytes 3932168 | tf_op jit(solution)/shard_map/ppermute | solution.py:24
  10.3 9.1 %copy-start = (f32[512,1280]{1,0:T(8,128)S(1)}, f32[512,1280]{1,0:T(8,128)}, u32[]{:S(2)}) copy-start(f32[512,1280]{1,0:T(8,128)} %refs_2_.1) | copy-start | bytes 7864324
  10.4 13.7 %copy-start.3 = (s32[4,17]{1,0:T(4,128)S(1)}, s32[4,17]{1,0:T(4,128)}, u32[]{:S(2)}) copy-start(s32[4,17]{1,0:T(4,128)} %pattern_ref.1) | copy-start | bytes 820
  10.4 4.9 %collective-permute-start.2 = (f32[256,1280]{1,0:T(8,128)S(1)}, f32[256,1280]{1,0:T(8,128)S(1)}, u32[]{:S(2)}, u32[]{:S(2)}) collective-permute-start(f32[256,1280]{1,0:T(8,128)S(1)} %get-tuple-element.21), channel_id=1, source_target_pairs={{0,1},{1,0},{2,3},{3,2},{4,5},{5,4},{6,7},{7,6},{8,9},{9,8},{10,11... | collective-permute-start | bytes 3932168 | tf_op jit(solution)/shard_map/ppermute | solution.py:24
  15.4 8.0 %collective-permute-start.5 = (f32[128,256]{1,0:T(8,128)S(1)}, f32[128,256]{1,0:T(8,128)S(1)}, u32[]{:S(2)}, u32[]{:S(2)}) collective-permute-start(f32[128,256]{1,0:T(8,128)S(1)} %slice.33), channel_id=1, source_target_pairs={{255,9},{0,246},{15,25},{16,6},{31,41},{32,22},{47,57},{48,38},{63... | collective-permute-start | bytes 393224 | tf_op jit(solution)/shard_map/ppermute | solution.py:187
  19.5 7.1 %collective-permute-start.3 = (f32[128,256]{1,0:T(8,128)S(1)}, f32[128,256]{1,0:T(8,128)S(1)}, u32[]{:S(2)}, u32[]{:S(2)}) collective-permute-start(f32[128,256]{1,0:T(8,128)S(1)} %slice.32), channel_id=1, source_target_pairs={{254,14},{1,241},{62,78},{65,49},{126,142},{129,113},{190,206},{19... | collective-permute-start | bytes 393224 | tf_op jit(solution)/shard_map/ppermute | solution.py:189
  23.4 4.7 %collective-permute-start.6 = (f32[128,256]{1,0:T(8,128)S(1)}, f32[128,256]{1,0:T(8,128)S(1)}, u32[]{:S(2)}, u32[]{:S(2)}) collective-permute-start(f32[128,256]{1,0:T(8,128)S(1)} %collective-permute-done.5), channel_id=1, source_target_pairs={{9,3},{246,252},{25,19},{6,12},{41,35},{22,28},{57,51},{38,44},{73... | collective-permute-start | bytes 393224 | tf_op jit(solution)/shard_map/ppermute | solution.py:187
  26.2 3.2 %copy-start.2 = (f32[512,1280]{1,0:T(8,128)S(1)}, f32[512,1280]{1,0:T(8,128)}, u32[]{:S(2)}) copy-start(f32[512,1280]{1,0:T(8,128)} %refs_6_.1) | copy-start | bytes 7864324
  26.5 33.7 %collective-permute-start.13 = (f32[512,1024]{1,0:T(8,128)S(1)}, f32[512,1024]{1,0:T(8,128)S(1)}, u32[]{:S(2)}, u32[]{:S(2)}) collective-permute-start(f32[512,1024]{1,0:T(8,128)S(1)} %slice.43), channel_id=1, source_target_pairs={{1,2},{2,1},{3,4},{4,3},{5,6},{6,5},{7,8},{8,7},{9,10},{10,9},{11,... | collective-permute-start | bytes 6291464 | tf_op jit(solution)/shard_map/ppermute | solution.py:24
  26.6 9.7 %collective-permute-start.4 = (f32[128,256]{1,0:T(8,128)S(1)}, f32[128,256]{1,0:T(8,128)S(1)}, u32[]{:S(2)}, u32[]{:S(2)}) collective-permute-start(f32[128,256]{1,0:T(8,128)S(1)} %collective-permute-done.3), channel_id=1, source_target_pairs={{14,0},{241,255},{78,64},{49,63},{142,128},{113,127},{206,192},{17... | collective-permute-start | bytes 393224 | tf_op jit(solution)/shard_map/ppermute | solution.py:189
  28.1 9.2 %collective-permute-start.7 = (f32[128,256]{1,0:T(8,128)S(1)}, f32[128,256]{1,0:T(8,128)S(1)}, u32[]{:S(2)}, u32[]{:S(2)}) collective-permute-start(f32[128,256]{1,0:T(8,128)S(1)} %collective-permute-done.6), channel_id=1, source_target_pairs={{3,0},{252,255},{19,16},{12,15},{35,32},{28,31},{51,48},{44,47},{6... | collective-permute-start | bytes 393224 | tf_op jit(solution)/shard_map/ppermute | solution.py:187
  37.9 3.1 %collective-permute-start.8 = (f32[256,1280]{1,0:T(8,128)S(1)}, f32[256,1280]{1,0:T(8,128)S(1)}, u32[]{:S(2)}, u32[]{:S(2)}) collective-permute-start(f32[256,1280]{1,0:T(8,128)S(1)} %get-tuple-element.19), channel_id=1, source_target_pairs={{0,1},{1,0},{2,3},{3,2},{4,5},{5,4},{6,7},{7,6},{8,9},{9,8},{10,11... | collective-permute-start | bytes 3932168 | tf_op jit(solution)/shard_map/ppermute | solution.py:24
  38.0 11.5 %collective-permute-start.9 = (f32[256,1280]{1,0:T(8,128)S(1)}, f32[256,1280]{1,0:T(8,128)S(1)}, u32[]{:S(2)}, u32[]{:S(2)}) collective-permute-start(f32[256,1280]{1,0:T(8,128)S(1)} %get-tuple-element.20), channel_id=1, source_target_pairs={{0,1},{1,0},{2,3},{3,2},{4,5},{5,4},{6,7},{7,6},{8,9},{9,8},{10,11... | collective-permute-start | bytes 3932168 | tf_op jit(solution)/shard_map/ppermute | solution.py:24
  38.5 24.6 %collective-permute-start.12 = (f32[128,256]{1,0:T(8,128)S(1)}, f32[128,256]{1,0:T(8,128)S(1)}, u32[]{:S(2)}, u32[]{:S(2)}) collective-permute-start(f32[128,256]{1,0:T(8,128)S(1)} %slice.42), channel_id=1, source_target_pairs={{15,16},{16,15},{31,32},{32,31},{47,48},{48,47},{79,80},{80,79},{9... | collective-permute-start | bytes 393224 | tf_op jit(solution)/shard_map/ppermute | solution.py:205
  39.2 23.9 %collective-permute-start.11 = (f32[256,256]{1,0:T(8,128)S(1)}, f32[256,256]{1,0:T(8,128)S(1)}, u32[]{:S(2)}, u32[]{:S(2)}) collective-permute-start(f32[256,256]{1,0:T(8,128)S(1)} %slice.41), channel_id=1, source_target_pairs={{1,2},{2,1},{3,4},{4,3},{5,6},{6,5},{7,8},{8,7},{9,10},{10,9},{11,... | collective-permute-start | bytes 786440 | tf_op jit(solution)/shard_map/ppermute | solution.py:204
  41.0 22.1 %collective-permute-start.10 = (f32[256,256]{1,0:T(8,128)S(1)}, f32[256,256]{1,0:T(8,128)S(1)}, u32[]{:S(2)}, u32[]{:S(2)}) collective-permute-start(f32[256,256]{1,0:T(8,128)S(1)} %slice.40), channel_id=1, source_target_pairs={{1,2},{2,1},{3,4},{4,3},{5,6},{6,5},{7,8},{8,7},{9,10},{10,9},{11,... | collective-permute-start | bytes 786440 | tf_op jit(solution)/shard_map/ppermute | solution.py:24

commit v6 on v5

--- a/solution.py
+++ b/solution.py
@@ -115,26 +115,35 @@
     )(*args)
 
 
-def joined(pieces):
-    if len(pieces) == 1:
-        return pieces[0]
-    rest, inner, short = pieces
+def row_halves(refs, here):
+    if len(refs) == 1:
+        half = refs[0].shape[0] // 2
+        return refs[0][:half, here], refs[0][half:, here]
+    rest, inner, short = [ref[:, here] for ref in refs]
     cut = short.shape[0]
-    return jnp.concatenate([rest, inner[:cut] + short, inner[cut:]], 0)
+    return rest, jnp.concatenate([inner[:cut] + short, inner[cut:]], 0)
 
 
 def last_kernel(start, step, count, *refs):
     high_ref, low_ref, acc_ref = refs[:3]
     block_refs = refs[3 : 3 + count]
     out_ref, stage, sems = refs[-3:]
+    half = acc_ref.shape[0] // 2
+    odd = lax.rem(lax.axis_index(AXIS), 2)
+    full = pl.ds(pl.multiple_of(odd * half, half), half)
+    part = pl.ds(pl.multiple_of((1 - odd) * half, half), half)
+    dot = functools.partial(jnp.dot, preferred_element_type=jnp.float32)
     copies = []
     for i in range(stage.shape[1] // step):
         here = slice(i * step, i * step + step)
         there = slice(start + i * step, start + i * step + step)
-        th, tl = split(joined([ref[:, here] for ref in block_refs]))
-        vh, vl = high_ref[BEYOND], low_ref[BEYOND]
-        dot = functools.partial(jnp.dot, preferred_element_type=jnp.float32)
-        stage[:, here] = acc_ref[:, there] + (dot(vh, th) + (dot(vh, tl) + dot(vl, th)))
+        upper, lower = row_halves(block_refs, here)
+        th, tl = split(jnp.concatenate([upper, lower], 0))
+        vh, vl = high_ref[BEYOND, full], low_ref[BEYOND, full]
+        stage[full, here] = acc_ref[full, there] + (dot(vh, th) + (dot(vh, tl) + dot(vl, th)))
+        th, tl = split(jnp.where(odd == 1, upper, lower))
+        vh, vl = high_ref[BEYOND, part, part], low_ref[BEYOND, part, part]
+        stage[part, here] = acc_ref[part, there] + (dot(vh, th) + (dot(vh, tl) + dot(vl, th)))
         copies.append(pltpu.make_async_copy(stage.at[:, here], out_ref.at[:, there], sems.at[i]))
         copies[-1].start()
     for copy in copies:
@@ -192,8 +201,7 @@
 
 def per_device(integrals, tile_pattern, amplitudes, residual_in):
     rows, width = amplitudes.shape
-    deep = 128
-    cut, first, second = 1024, rows - 2 * deep, rows - deep
+    cut, first, second = 1024, rows - 256, rows - 144
     facing = exchange(amplitudes, 1)
     high, low = align(integrals, tile_pattern)
     n = rows // 2

time: 64.7 us -> 64.5 us (level)
  Pallas kernels: 18.2 us -> 17.5 us
    ppermute x3, waiting for transfers between devices: 4.23 us -> 5.63 us  [detours(): one = lax.ppermute(one, AXIS, pairs)]
    ppermute x7, waiting for transfers between devices: 10.2 us -> 9.14 us  [exchange(): return lax.ppermute(value, AXIS, pairs)]
    pallas_call x2, Pallas kernels: 4.29 us -> 3.6 us  [add_last(): pl.pallas_call(functools.partial(last_kernel, start, step, len(blocks)),...]
  transfers between devices with their start and end apart: 14 -> 14, of which waited for: 8 -> 8; matrix products, arithmetic and copies ran while one was open for 5% -> 5% of each run, Pallas kernels for 26% -> 25%
where the time goes in v6:
time: 64.5 us; the launch traced here: 64.3 us
  starting transfers between devices  27.9 us (43%)
  Pallas kernels  17.5 us (27%)
  waiting for transfers between devices  15.7 us (24%)
  local copies, waits for them, and re-layouts  2.76 us (4%)
    ppermute x7, starting transfers between devices, exchange(): return lax.ppermute(value, AXIS, pairs)  18.4 us
    pallas_call x2, Pallas kernels, add_products(): pl.pallas_call(functools.partial(add_kernel, n), grid=(width // cols,), i...  11.8 us
    ppermute x7, waiting for transfers between devices, exchange(): return lax.ppermute(value, AXIS, pairs)  9.14 us
    ppermute x3, starting transfers between devices, detours(): one = lax.ppermute(one, AXIS, pairs)  6.06 us
    ppermute x3, waiting for transfers between devices, detours(): one = lax.ppermute(one, AXIS, pairs)  5.63 us
    pallas_call x2, Pallas kernels, add_last(): pl.pallas_call(functools.partial(last_kernel, start, step, len(blocks)),...  3.6 us
    pallas_call x1, Pallas kernels, align(): pl.pallas_call(functools.partial(align_kernel, tiles), grid=(tiles,), in_...  2.1 us
    ppermute x2, starting transfers between devices, detours(): two = lax.ppermute(two, AXIS, pairs)  2.09 us
  transfers between devices with their start and end apart: 14, of which 8 were waited for; matrix products, arithmetic and copies ran while one was open for 5% of the time, Pallas kernels for 25%

profile of v6, /device:TPU:0, one launch (start us, length us, event | category | flops | bytes accessed | tf_op | source)
XLA Modules:
  0.0 64.3 jit_solution(1545548949270352585)
XLA Ops:
  0.0 8.2 %collective-permute-start = (f32[512,1280]{1,0:T(8,128)}, f32[512,1280]{1,0:T(8,128)S(1)}, u32[]{:S(2)}, u32[]{:S(2)}) collective-permute-start(f32[512,1280]{1,0:T(8,128)} %refs_2_.1), channel_id=1, source_target_pairs={{1,2},{2,1},{3,4},{4,3},{5,6},{6,5},{7,8},{8,7},{9,10},{10,9},{11,... | collective-permute-start | bytes 7864328 | tf_op jit(solution)/shard_map/ppermute | solution.py:24
  8.2 0.0 copy-start.1
  8.2 2.0 %fusion.1 = (f32[256,1280]{1,0:T(8,128)S(1)}, f32[256,1280]{1,0:T(8,128)S(1)}) fusion(f32[512,1280]{1,0:T(8,128)} %refs_2_.1), kind=kLoop, calls=%fused_computation.5 | loop fusion | bytes 5242880 | tf_op jit(solution)/shard_map/slice | solution.py:208
  10.2 0.1 collective-permute-start.1
  10.3 0.0 copy-start
  10.4 0.0 copy-start.3
  10.4 0.5 collective-permute-start.2
  10.8 2.5 %collective-permute-done.1 = f32[256,1280]{1,0:T(8,128)S(1)} collective-permute-done((f32[256,1280]{1,0:T(8,128)S(1)}, f32[256,1280]{1,0:T(8,128)S(1)}, u32[]{:S(2)}, u32[]{:S(2)}) %collective-permute-start.1) | collective-permute-done | bytes 1310752 | tf_op jit(solution)/shard_map/ppermute | solution.py:24
  13.4 0.1 constant_dynamic-update-slice_fusion.1
  13.5 1.8 %collective-permute-done.2 = f32[256,1280]{1,0:T(8,128)S(1)} collective-permute-done((f32[256,1280]{1,0:T(8,128)S(1)}, f32[256,1280]{1,0:T(8,128)S(1)}, u32[]{:S(2)}, u32[]{:S(2)}) %collective-permute-start.2) | collective-permute-done | bytes 1310752 | tf_op jit(solution)/shard_map/ppermute | solution.py:24
  15.2 0.1 constant_dynamic-update-slice_fusion.refs_5_
  15.4 4.1 %collective-permute-start.5 = (f32[144,256]{1,0:T(8,128)S(1)}, f32[144,256]{1,0:T(8,128)S(1)}, u32[]{:S(2)}, u32[]{:S(2)}) collective-permute-start(f32[144,256]{1,0:T(8,128)S(1)} %slice.33), channel_id=1, source_target_pairs={{255,9},{0,246},{15,25},{16,6},{31,41},{32,22},{47,57},{48,38},{63... | collective-permute-start | bytes 442376 | tf_op jit(solution)/shard_map/ppermute | solution.py:196
  19.5 4.3 %collective-permute-done.5 = f32[144,256]{1,0:T(8,128)S(1)} collective-permute-done((f32[144,256]{1,0:T(8,128)S(1)}, f32[144,256]{1,0:T(8,128)S(1)}, u32[]{:S(2)}, u32[]{:S(2)}) %collective-permute-start.5) | collective-permute-done | bytes 147488 | tf_op jit(solution)/shard_map/ppermute | solution.py:196
  23.8 0.7 %collective-permute-start.6 = (f32[144,256]{1,0:T(8,128)S(1)}, f32[144,256]{1,0:T(8,128)S(1)}, u32[]{:S(2)}, u32[]{:S(2)}) collective-permute-start(f32[144,256]{1,0:T(8,128)S(1)} %collective-permute-done.5), channel_id=1, source_target_pairs={{9,3},{246,252},{25,19},{6,12},{41,35},{22,28},{57,51},{38,44},{73... | collective-permute-start | bytes 442376 | tf_op jit(solution)/shard_map/ppermute | solution.py:196
  24.4 0.0 copy-done
  24.4 0.7 %collective-permute-start.3 = (f32[112,256]{1,0:T(8,128)S(1)}, f32[112,256]{1,0:T(8,128)S(1)}, u32[]{:S(2)}, u32[]{:S(2)}) collective-permute-start(f32[112,256]{1,0:T(8,128)S(1)} %slice.32), channel_id=1, source_target_pairs={{254,14},{1,241},{62,78},{65,49},{126,142},{129,113},{190,206},{19... | collective-permute-start | bytes 344072 | tf_op jit(solution)/shard_map/ppermute | solution.py:198
  25.1 0.0 copy-done.1
  25.1 0.0 copy-done.3
  25.1 2.1 %align.1 = (bf16[5,512,512]{2,1,0:T(8,128)(2,1)S(1)}, bf16[5,512,512]{2,1,0:T(8,128)(2,1)S(1)}) custom-call(s32[4,17]{1,0:T(4,128)S(1)} %copy-done.3, f32[512,2176]{1,0:T(8,128)S(1)} %copy-done.1), custom_call_target="tpu_custom_call" | custom-call | flops 2621440 | bytes 10000000 | tf_op jit(solution)/shard_map/align/pallas_call | solution.py:55
  27.2 0.0 copy-start.2
  27.3 0.3 slice.43
  27.6 0.1 collective-permute-start.13
  27.7 0.0 collective-permute-done.3
  27.7 1.4 %collective-permute-start.4 = (f32[112,256]{1,0:T(8,128)S(1)}, f32[112,256]{1,0:T(8,128)S(1)}, u32[]{:S(2)}, u32[]{:S(2)}) collective-permute-start(f32[112,256]{1,0:T(8,128)S(1)} %collective-permute-done.3), channel_id=1, source_target_pairs={{14,0},{241,255},{78,64},{49,63},{142,128},{113,127},{206,192},{17... | collective-permute-start | bytes 344072 | tf_op jit(solution)/shard_map/ppermute | solution.py:198
  29.1 0.0 collective-permute-done.6
  29.1 1.3 %collective-permute-start.7 = (f32[144,256]{1,0:T(8,128)S(1)}, f32[144,256]{1,0:T(8,128)S(1)}, u32[]{:S(2)}, u32[]{:S(2)}) collective-permute-start(f32[144,256]{1,0:T(8,128)S(1)} %collective-permute-done.6), channel_id=1, source_target_pairs={{3,0},{252,255},{19,16},{12,15},{35,32},{28,31},{51,48},{44,47},{6... | collective-permute-start | bytes 442376 | tf_op jit(solution)/shard_map/ppermute | solution.py:196
  30.4 0.0 copy-done.2
  30.4 5.7 %near.1.refs_9_ = f32[512,1280]{1,0:T(8,128)S(1)} custom-call(bf16[5,512,512]{2,1,0:T(8,128)(2,1)S(1)} %get-tuple-element.12.refs_0_.refs_3_.refs_6_, bf16[5,512,512]{2,1,0:T(8,128)(2,1)S(1)} %get-tuple-element.13.refs_1_.refs_4_.refs_7_, f32[512,1280]{1,0:T(8,128)S(1)} %copy-done, bf16[5,512,512]{2,1,0:T(8,128)(2,1)S(1)} %get-tuple-element.12.refs_0_.refs_3_.refs_6_, ...), custom_call_target="tpu_custom_call" | custom-call | flops 2013265920 | bytes 1 | tf_op jit(solution)/shard_map/near/pallas_call | solution.py:106
  36.1 0.9 %collective-permute-done.4 = f32[112,256]{1,0:T(8,128)S(1)} collective-permute-done((f32[112,256]{1,0:T(8,128)S(1)}, f32[112,256]{1,0:T(8,128)S(1)}, u32[]{:S(2)}, u32[]{:S(2)}) %collective-permute-start.4) | collective-permute-done | bytes 114720 | tf_op jit(solution)/shard_map/ppermute | solution.py:198
  37.0 1.4 %collective-permute-done.7 = f32[144,256]{1,0:T(8,128)S(1)} collective-permute-done((f32[144,256]{1,0:T(8,128)S(1)}, f32[144,256]{1,0:T(8,128)S(1)}, u32[]{:S(2)}, u32[]{:S(2)}) %collective-permute-start.7) | collective-permute-done | bytes 147488 | tf_op jit(solution)/shard_map/ppermute | solution.py:196
  38.4 0.0 collective-permute-done.refs_2_
  38.4 0.2 fusion
  38.6 0.1 collective-permute-start.8
  38.7 0.5 collective-permute-start.9
  39.2 0.7 %collective-permute-start.12 = (f32[112,256]{1,0:T(8,128)S(1)}, f32[112,256]{1,0:T(8,128)S(1)}, u32[]{:S(2)}, u32[]{:S(2)}) collective-permute-start(f32[112,256]{1,0:T(8,128)S(1)} %slice.42), channel_id=1, source_target_pairs={{15,16},{16,15},{31,32},{32,31},{47,48},{48,47},{79,80},{80,79},{9... | collective-permute-start | bytes 344072 | tf_op jit(solution)/shard_map/ppermute | solution.py:213
  39.9 0.7 %collective-permute-start.11 = (f32[256,256]{1,0:T(8,128)S(1)}, f32[256,256]{1,0:T(8,128)S(1)}, u32[]{:S(2)}, u32[]{:S(2)}) collective-permute-start(f32[256,256]{1,0:T(8,128)S(1)} %slice.41), channel_id=1, source_target_pairs={{1,2},{2,1},{3,4},{4,3},{5,6},{6,5},{7,8},{8,7},{9,10},{10,9},{11,... | collective-permute-start | bytes 786440 | tf_op jit(solution)/shard_map/ppermute | solution.py:212
  40.6 1.1 %collective-permute-done.8 = f32[256,1280]{1,0:T(8,128)S(1)} collective-permute-done((f32[256,1280]{1,0:T(8,128)S(1)}, f32[256,1280]{1,0:T(8,128)S(1)}, u32[]{:S(2)}, u32[]{:S(2)}) %collective-permute-start.8) | collective-permute-done | bytes 1310752 | tf_op jit(solution)/shard_map/ppermute | solution.py:24
  41.7 8.9 %collective-permute-start.10 = (f32[256,256]{1,0:T(8,128)S(1)}, f32[256,256]{1,0:T(8,128)S(1)}, u32[]{:S(2)}, u32[]{:S(2)}) collective-permute-start(f32[256,256]{1,0:T(8,128)S(1)} %slice.40), channel_id=1, source_target_pairs={{1,2},{2,1},{3,4},{4,3},{5,6},{6,5},{7,8},{8,7},{9,10},{10,9},{11,... | collective-permute-start | bytes 786440 | tf_op jit(solution)/shard_map/ppermute | solution.py:24
  50.6 0.0 collective-permute-done.9
  50.6 0.2 pad_maximum_fusion.refs_5_
  50.8 6.2 %middle.1.refs_2_ = f32[512,1280]{1,0:T(8,128)S(1)} custom-call(bf16[5,512,512]{2,1,0:T(8,128)(2,1)S(1)} %get-tuple-element.12.refs_0_.refs_3_.refs_6_, bf16[5,512,512]{2,1,0:T(8,128)(2,1)S(1)} %get-tuple-element.13.refs_1_.refs_4_.refs_7_, f32[512,1280]{1,0:T(8,128)S(1)} %collective-permute-done.refs_2_, ...), custom_call_target="tpu_custom_call" | custom-call | flops 1 | bytes 1 | tf_op jit(solution)/shard_map/middle/pallas_call | solution.py:106
  57.0 3.3 %collective-permute-done.13.refs_3_ = f32[512,1024]{1,0:T(8,128)S(1)} collective-permute-done((f32[512,1024]{1,0:T(8,128)S(1)}, f32[512,1024]{1,0:T(8,128)S(1)}, u32[]{:S(2)}, u32[]{:S(2)}) %collective-permute-start.13) | collective-permute-done | bytes 2097184 | tf_op jit(solution)/shard_map/ppermute | solution.py:24
  60.2 2.3 %last0.1.refs_6_ = f32[512,1280]{1,0:T(8,128)} custom-call(bf16[5,512,512]{2,1,0:T(8,128)(2,1)S(1)} %get-tuple-element.12.refs_0_.refs_3_.refs_6_, bf16[5,512,512]{2,1,0:T(8,128)(2,1)S(1)} %get-tuple-element.13.refs_1_.refs_4_.refs_7_, f32[512,1280]{1,0:T(8,128)S(1)} %middle.1.refs_2_, f32[512,1024]{1,0:T(8,128)S(1)} %collective-permute-done.13.refs_3_), custom_call_target="tpu_custom_call" | custom-call | flops 1 | bytes 1 | tf_op jit(solution)/shard_map/last0/pallas_call | solution.py:163
  62.5 0.0 collective-permute-done.12.refs_5_
  62.6 0.0 collective-permute-done.11.refs_4_
  62.6 0.5 collective-permute-done.10.refs_3_
  63.0 1.3 %last1.1 = f32[512,1280]{1,0:T(8,128)} custom-call(bf16[5,512,512]{2,1,0:T(8,128)(2,1)S(1)} %get-tuple-element.12.refs_0_.refs_3_.refs_6_, bf16[5,512,512]{2,1,0:T(8,128)(2,1)S(1)} %get-tuple-element.13.refs_1_.refs_4_.refs_7_, f32[512,1280]{1,0:T(8,128)S(1)} %middle.1.refs_2_, ...), custom_call_target="tpu_custom_call", output_to_operand_aliasing={{}: (6, {})} | custom-call | flops 1 | bytes 1 | tf_op jit(solution)/shard_map/last1/pallas_call | solution.py:163
  (6 shorter events, 0.1 us)
Async XLA Ops:
  0.0 38.4 %collective-permute-start = (f32[512,1280]{1,0:T(8,128)}, f32[512,1280]{1,0:T(8,128)S(1)}, u32[]{:S(2)}, u32[]{:S(2)}) collective-permute-start(f32[512,1280]{1,0:T(8,128)} %refs_2_.1), channel_id=1, source_target_pairs={{1,2},{2,1},{3,4},{4,3},{5,6},{6,5},{7,8},{8,7},{9,10},{10,9},{11,... | collective-permute-start | bytes 7864328 | tf_op jit(solution)/shard_map/ppermute | solution.py:24
  8.2 16.9 %copy-start.1 = (f32[512,2176]{1,0:T(8,128)S(1)}, f32[512,2176]{1,0:T(8,128)}, u32[]{:S(2)}) copy-start(f32[512,2176]{1,0:T(8,128)} %v_ref.1) | copy-start | bytes 13369348
  10.2 3.1 %collective-permute-start.1 = (f32[256,1280]{1,0:T(8,128)S(1)}, f32[256,1280]{1,0:T(8,128)S(1)}, u32[]{:S(2)}, u32[]{:S(2)}) collective-permute-start(f32[256,1280]{1,0:T(8,128)S(1)} %get-tuple-element.22), channel_id=1, source_target_pairs={{0,1},{1,0},{2,3},{3,2},{4,5},{5,4},{6,7},{7,6},{8,9},{9,8},{10,11... | collective-permute-start | bytes 3932168 | tf_op jit(solution)/shard_map/ppermute | solution.py:24
  10.3 14.1 %copy-start = (f32[512,1280]{1,0:T(8,128)S(1)}, f32[512,1280]{1,0:T(8,128)}, u32[]{:S(2)}) copy-start(f32[512,1280]{1,0:T(8,128)} %refs_2_.1) | copy-start | bytes 7864324
  10.4 14.8 %copy-start.3 = (s32[4,17]{1,0:T(4,128)S(1)}, s32[4,17]{1,0:T(4,128)}, u32[]{:S(2)}) copy-start(s32[4,17]{1,0:T(4,128)} %pattern_ref.1) | copy-start | bytes 820
  10.4 4.9 %collective-permute-start.2 = (f32[256,1280]{1,0:T(8,128)S(1)}, f32[256,1280]{1,0:T(8,128)S(1)}, u32[]{:S(2)}, u32[]{:S(2)}) collective-permute-start(f32[256,1280]{1,0:T(8,128)S(1)} %get-tuple-element.21), channel_id=1, source_target_pairs={{0,1},{1,0},{2,3},{3,2},{4,5},{5,4},{6,7},{7,6},{8,9},{9,8},{10,11... | collective-permute-start | bytes 3932168 | tf_op jit(solution)/shard_map/ppermute | solution.py:24
  15.4 8.4 %collective-permute-start.5 = (f32[144,256]{1,0:T(8,128)S(1)}, f32[144,256]{1,0:T(8,128)S(1)}, u32[]{:S(2)}, u32[]{:S(2)}) collective-permute-start(f32[144,256]{1,0:T(8,128)S(1)} %slice.33), channel_id=1, source_target_pairs={{255,9},{0,246},{15,25},{16,6},{31,41},{32,22},{47,57},{48,38},{63... | collective-permute-start | bytes 442376 | tf_op jit(solution)/shard_map/ppermute | solution.py:196
  23.8 5.4 %collective-permute-start.6 = (f32[144,256]{1,0:T(8,128)S(1)}, f32[144,256]{1,0:T(8,128)S(1)}, u32[]{:S(2)}, u32[]{:S(2)}) collective-permute-start(f32[144,256]{1,0:T(8,128)S(1)} %collective-permute-done.5), channel_id=1, source_target_pairs={{9,3},{246,252},{25,19},{6,12},{41,35},{22,28},{57,51},{38,44},{73... | collective-permute-start | bytes 442376 | tf_op jit(solution)/shard_map/ppermute | solution.py:196
  24.4 3.2 %collective-permute-start.3 = (f32[112,256]{1,0:T(8,128)S(1)}, f32[112,256]{1,0:T(8,128)S(1)}, u32[]{:S(2)}, u32[]{:S(2)}) collective-permute-start(f32[112,256]{1,0:T(8,128)S(1)} %slice.32), channel_id=1, source_target_pairs={{254,14},{1,241},{62,78},{65,49},{126,142},{129,113},{190,206},{19... | collective-permute-start | bytes 344072 | tf_op jit(solution)/shard_map/ppermute | solution.py:198
  27.2 3.2 %copy-start.2 = (f32[512,1280]{1,0:T(8,128)S(1)}, f32[512,1280]{1,0:T(8,128)}, u32[]{:S(2)}) copy-start(f32[512,1280]{1,0:T(8,128)} %refs_6_.1) | copy-start | bytes 7864324
  27.6 32.7 %collective-permute-start.13 = (f32[512,1024]{1,0:T(8,128)S(1)}, f32[512,1024]{1,0:T(8,128)S(1)}, u32[]{:S(2)}, u32[]{:S(2)}) collective-permute-start(f32[512,1024]{1,0:T(8,128)S(1)} %slice.43), channel_id=1, source_target_pairs={{1,2},{2,1},{3,4},{4,3},{5,6},{6,5},{7,8},{8,7},{9,10},{10,9},{11,... | collective-permute-start | bytes 6291464 | tf_op jit(solution)/shard_map/ppermute | solution.py:24
  27.7 9.3 %collective-permute-start.4 = (f32[112,256]{1,0:T(8,128)S(1)}, f32[112,256]{1,0:T(8,128)S(1)}, u32[]{:S(2)}, u32[]{:S(2)}) collective-permute-start(f32[112,256]{1,0:T(8,128)S(1)} %collective-permute-done.3), channel_id=1, source_target_pairs={{14,0},{241,255},{78,64},{49,63},{142,128},{113,127},{206,192},{17... | collective-permute-start | bytes 344072 | tf_op jit(solution)/shard_map/ppermute | solution.py:198
  29.1 9.2 %collective-permute-start.7 = (f32[144,256]{1,0:T(8,128)S(1)}, f32[144,256]{1,0:T(8,128)S(1)}, u32[]{:S(2)}, u32[]{:S(2)}) collective-permute-start(f32[144,256]{1,0:T(8,128)S(1)} %collective-permute-done.6), channel_id=1, source_target_pairs={{3,0},{252,255},{19,16},{12,15},{35,32},{28,31},{51,48},{44,47},{6... | collective-permute-start | bytes 442376 | tf_op jit(solution)/shard_map/ppermute | solution.py:196
  38.6 3.1 %collective-permute-start.8 = (f32[256,1280]{1,0:T(8,128)S(1)}, f32[256,1280]{1,0:T(8,128)S(1)}, u32[]{:S(2)}, u32[]{:S(2)}) collective-permute-start(f32[256,1280]{1,0:T(8,128)S(1)} %get-tuple-element.19), channel_id=1, source_target_pairs={{0,1},{1,0},{2,3},{3,2},{4,5},{5,4},{6,7},{7,6},{8,9},{9,8},{10,11... | collective-permute-start | bytes 3932168 | tf_op jit(solution)/shard_map/ppermute | solution.py:24
  38.7 11.9 %collective-permute-start.9 = (f32[256,1280]{1,0:T(8,128)S(1)}, f32[256,1280]{1,0:T(8,128)S(1)}, u32[]{:S(2)}, u32[]{:S(2)}) collective-permute-start(f32[256,1280]{1,0:T(8,128)S(1)} %get-tuple-element.20), channel_id=1, source_target_pairs={{0,1},{1,0},{2,3},{3,2},{4,5},{5,4},{6,7},{7,6},{8,9},{9,8},{10,11... | collective-permute-start | bytes 3932168 | tf_op jit(solution)/shard_map/ppermute | solution.py:24
  39.2 23.4 %collective-permute-start.12 = (f32[112,256]{1,0:T(8,128)S(1)}, f32[112,256]{1,0:T(8,128)S(1)}, u32[]{:S(2)}, u32[]{:S(2)}) collective-permute-start(f32[112,256]{1,0:T(8,128)S(1)} %slice.42), channel_id=1, source_target_pairs={{15,16},{16,15},{31,32},{32,31},{47,48},{48,47},{79,80},{80,79},{9... | collective-permute-start | bytes 344072 | tf_op jit(solution)/shard_map/ppermute | solution.py:213
  39.9 22.7 %collective-permute-start.11 = (f32[256,256]{1,0:T(8,128)S(1)}, f32[256,256]{1,0:T(8,128)S(1)}, u32[]{:S(2)}, u32[]{:S(2)}) collective-permute-start(f32[256,256]{1,0:T(8,128)S(1)} %slice.41), channel_id=1, source_target_pairs={{1,2},{2,1},{3,4},{4,3},{5,6},{6,5},{7,8},{8,7},{9,10},{10,9},{11,... | collective-permute-start | bytes 786440 | tf_op jit(solution)/shard_map/ppermute | solution.py:212
  41.7 21.3 %collective-permute-start.10 = (f32[256,256]{1,0:T(8,128)S(1)}, f32[256,256]{1,0:T(8,128)S(1)}, u32[]{:S(2)}, u32[]{:S(2)}) collective-permute-start(f32[256,256]{1,0:T(8,128)S(1)} %slice.40), channel_id=1, source_target_pairs={{1,2},{2,1},{3,4},{4,3},{5,6},{6,5},{7,8},{8,7},{9,10},{10,9},{11,... | collective-permute-start | bytes 786440 | tf_op jit(solution)/shard_map/ppermute | solution.py:24

commit v7 on v6

--- a/solution.py
+++ b/solution.py
@@ -138,13 +138,15 @@
         here = slice(i * step, i * step + step)
         there = slice(start + i * step, start + i * step + step)
         upper, lower = row_halves(block_refs, here)
+        th, tl = split(jnp.where(odd == 1, upper, lower))
+        vh, vl = high_ref[BEYOND, part, part], low_ref[BEYOND, part, part]
+        stage[part, here] = acc_ref[part, there] + (dot(vh, th) + (dot(vh, tl) + dot(vl, th)))
+        copies.append(pltpu.make_async_copy(stage.at[part, here], out_ref.at[part, there], sems.at[2 * i]))
+        copies[-1].start()
         th, tl = split(jnp.concatenate([upper, lower], 0))
         vh, vl = high_ref[BEYOND, full], low_ref[BEYOND, full]
         stage[full, here] = acc_ref[full, there] + (dot(vh, th) + (dot(vh, tl) + dot(vl, th)))
-        th, tl = split(jnp.where(odd == 1, upper, lower))
-        vh, vl = high_ref[BEYOND, part, part], low_ref[BEYOND, part, part]
-        stage[part, here] = acc_ref[part, there] + (dot(vh, th) + (dot(vh, tl) + dot(vl, th)))
-        copies.append(pltpu.make_async_copy(stage.at[:, here], out_ref.at[:, there], sems.at[i]))
+        copies.append(pltpu.make_async_copy(stage.at[full, here], out_ref.at[full, there], sems.at[2 * i + 1]))
         copies[-1].start()
     for copy in copies:
         copy.wait()
@@ -166,7 +168,7 @@
         out_specs=pl.BlockSpec(memory_space=pl.ANY),
         out_shape=jax.ShapeDtypeStruct(acc.shape, acc.dtype),
         input_output_aliases=aliases,
-        scratch_shapes=[pltpu.VMEM((rows, width), jnp.float32), pltpu.SemaphoreType.DMA((width // step,))],
+        scratch_shapes=[pltpu.VMEM((rows, width), jnp.float32), pltpu.SemaphoreType.DMA((2 * width // step,))],
         compiler_params=pltpu.CompilerParams(vmem_limit_bytes=16 * 2**20),
         cost_estimate=pl.CostEstimate(flops=1, bytes_accessed=1, transcendentals=0),
         name=name,

time: 64.5 us -> 64.4 us (level)
  transfers between devices with their start and end apart: 14 -> 14, of which waited for: 8 -> 8; matrix products, arithmetic and copies ran while one was open for 5% -> 5% of each run, Pallas kernels for 25% -> 26%
where the time goes in v7:
time: 64.4 us; the launch traced here: 64.3 us
  starting transfers between devices  27.9 us (43%)
  Pallas kernels  17.7 us (27%)
  waiting for transfers between devices  15.5 us (24%)
  local copies, waits for them, and re-layouts  2.76 us (4%)
    ppermute x7, starting transfers between devices, exchange(): return lax.ppermute(value, AXIS, pairs)  18.4 us
    pallas_call x2, Pallas kernels, add_products(): pl.pallas_call(functools.partial(add_kernel, n), grid=(width // cols,), i...  11.8 us
    ppermute x7, waiting for transfers between devices, exchange(): return lax.ppermute(value, AXIS, pairs)  8.93 us
    ppermute x3, starting transfers between devices, detours(): one = lax.ppermute(one, AXIS, pairs)  6.06 us
    ppermute x3, waiting for transfers between devices, detours(): one = lax.ppermute(one, AXIS, pairs)  5.63 us
    pallas_call x2, Pallas kernels, add_last(): pl.pallas_call(functools.partial(last_kernel, start, step, len(blocks)),...  3.75 us
    pallas_call x1, Pallas kernels, align(): pl.pallas_call(functools.partial(align_kernel, tiles), grid=(tiles,), in_...  2.1 us
    ppermute x2, starting transfers between devices, detours(): two = lax.ppermute(two, AXIS, pairs)  2.09 us
  transfers between devices with their start and end apart: 14, of which 8 were waited for; matrix products, arithmetic and copies ran while one was open for 5% of the time, Pallas kernels for 26%

profile of v7, /device:TPU:0, one launch (start us, length us, event | category | flops | bytes accessed | tf_op | source)
XLA Modules:
  0.0 64.3 jit_solution(15311158176566804359)
XLA Ops:
  0.0 8.2 %collective-permute-start = (f32[512,1280]{1,0:T(8,128)}, f32[512,1280]{1,0:T(8,128)S(1)}, u32[]{:S(2)}, u32[]{:S(2)}) collective-permute-start(f32[512,1280]{1,0:T(8,128)} %refs_2_.1), channel_id=1, source_target_pairs={{1,2},{2,1},{3,4},{4,3},{5,6},{6,5},{7,8},{8,7},{9,10},{10,9},{11,... | collective-permute-start | bytes 7864328 | tf_op jit(solution)/shard_map/ppermute | solution.py:24
  8.2 0.0 copy-start.1
  8.2 2.0 %fusion.1 = (f32[256,1280]{1,0:T(8,128)S(1)}, f32[256,1280]{1,0:T(8,128)S(1)}) fusion(f32[512,1280]{1,0:T(8,128)} %refs_2_.1), kind=kLoop, calls=%fused_computation.5 | loop fusion | bytes 5242880 | tf_op jit(solution)/shard_map/slice | solution.py:210
  10.2 0.1 collective-permute-start.1
  10.3 0.0 copy-start
  10.4 0.0 copy-start.3
  10.4 0.5 collective-permute-start.2
  10.8 2.5 %collective-permute-done.1 = f32[256,1280]{1,0:T(8,128)S(1)} collective-permute-done((f32[256,1280]{1,0:T(8,128)S(1)}, f32[256,1280]{1,0:T(8,128)S(1)}, u32[]{:S(2)}, u32[]{:S(2)}) %collective-permute-start.1) | collective-permute-done | bytes 1310752 | tf_op jit(solution)/shard_map/ppermute | solution.py:24
  13.4 0.1 constant_dynamic-update-slice_fusion.1
  13.5 1.8 %collective-permute-done.2 = f32[256,1280]{1,0:T(8,128)S(1)} collective-permute-done((f32[256,1280]{1,0:T(8,128)S(1)}, f32[256,1280]{1,0:T(8,128)S(1)}, u32[]{:S(2)}, u32[]{:S(2)}) %collective-permute-start.2) | collective-permute-done | bytes 1310752 | tf_op jit(solution)/shard_map/ppermute | solution.py:24
  15.2 0.1 constant_dynamic-update-slice_fusion.refs_5_
  15.4 4.1 %collective-permute-start.5 = (f32[144,256]{1,0:T(8,128)S(1)}, f32[144,256]{1,0:T(8,128)S(1)}, u32[]{:S(2)}, u32[]{:S(2)}) collective-permute-start(f32[144,256]{1,0:T(8,128)S(1)} %slice.33), channel_id=1, source_target_pairs={{255,9},{0,246},{15,25},{16,6},{31,41},{32,22},{47,57},{48,38},{63... | collective-permute-start | bytes 442376 | tf_op jit(solution)/shard_map/ppermute | solution.py:198
  19.5 4.3 %collective-permute-done.5 = f32[144,256]{1,0:T(8,128)S(1)} collective-permute-done((f32[144,256]{1,0:T(8,128)S(1)}, f32[144,256]{1,0:T(8,128)S(1)}, u32[]{:S(2)}, u32[]{:S(2)}) %collective-permute-start.5) | collective-permute-done | bytes 147488 | tf_op jit(solution)/shard_map/ppermute | solution.py:198
  23.8 0.7 %collective-permute-start.6 = (f32[144,256]{1,0:T(8,128)S(1)}, f32[144,256]{1,0:T(8,128)S(1)}, u32[]{:S(2)}, u32[]{:S(2)}) collective-permute-start(f32[144,256]{1,0:T(8,128)S(1)} %collective-permute-done.5), channel_id=1, source_target_pairs={{9,3},{246,252},{25,19},{6,12},{41,35},{22,28},{57,51},{38,44},{73... | collective-permute-start | bytes 442376 | tf_op jit(solution)/shard_map/ppermute | solution.py:198
  24.4 0.0 copy-done
  24.4 0.7 %collective-permute-start.3 = (f32[112,256]{1,0:T(8,128)S(1)}, f32[112,256]{1,0:T(8,128)S(1)}, u32[]{:S(2)}, u32[]{:S(2)}) collective-permute-start(f32[112,256]{1,0:T(8,128)S(1)} %slice.32), channel_id=1, source_target_pairs={{254,14},{1,241},{62,78},{65,49},{126,142},{129,113},{190,206},{19... | collective-permute-start | bytes 344072 | tf_op jit(solution)/shard_map/ppermute | solution.py:200
  25.1 0.0 copy-done.1
  25.1 0.0 copy-done.3
  25.1 2.1 %align.1 = (bf16[5,512,512]{2,1,0:T(8,128)(2,1)S(1)}, bf16[5,512,512]{2,1,0:T(8,128)(2,1)S(1)}) custom-call(s32[4,17]{1,0:T(4,128)S(1)} %copy-done.3, f32[512,2176]{1,0:T(8,128)S(1)} %copy-done.1), custom_call_target="tpu_custom_call" | custom-call | flops 2621440 | bytes 10000000 | tf_op jit(solution)/shard_map/align/pallas_call | solution.py:55
  27.2 0.0 copy-start.2
  27.3 0.3 slice.43
  27.6 0.1 collective-permute-start.13
  27.7 0.0 collective-permute-done.3
  27.7 1.4 %collective-permute-start.4 = (f32[112,256]{1,0:T(8,128)S(1)}, f32[112,256]{1,0:T(8,128)S(1)}, u32[]{:S(2)}, u32[]{:S(2)}) collective-permute-start(f32[112,256]{1,0:T(8,128)S(1)} %collective-permute-done.3), channel_id=1, source_target_pairs={{14,0},{241,255},{78,64},{49,63},{142,128},{113,127},{206,192},{17... | collective-permute-start | bytes 344072 | tf_op jit(solution)/shard_map/ppermute | solution.py:200
  29.1 0.0 collective-permute-done.6
  29.1 1.3 %collective-permute-start.7 = (f32[144,256]{1,0:T(8,128)S(1)}, f32[144,256]{1,0:T(8,128)S(1)}, u32[]{:S(2)}, u32[]{:S(2)}) collective-permute-start(f32[144,256]{1,0:T(8,128)S(1)} %collective-permute-done.6), channel_id=1, source_target_pairs={{3,0},{252,255},{19,16},{12,15},{35,32},{28,31},{51,48},{44,47},{6... | collective-permute-start | bytes 442376 | tf_op jit(solution)/shard_map/ppermute | solution.py:198
  30.4 0.0 copy-done.2
  30.4 5.7 %near.1.refs_9_ = f32[512,1280]{1,0:T(8,128)S(1)} custom-call(bf16[5,512,512]{2,1,0:T(8,128)(2,1)S(1)} %get-tuple-element.12.refs_0_.refs_3_.refs_6_, bf16[5,512,512]{2,1,0:T(8,128)(2,1)S(1)} %get-tuple-element.13.refs_1_.refs_4_.refs_7_, f32[512,1280]{1,0:T(8,128)S(1)} %copy-done, bf16[5,512,512]{2,1,0:T(8,128)(2,1)S(1)} %get-tuple-element.12.refs_0_.refs_3_.refs_6_, ...), custom_call_target="tpu_custom_call" | custom-call | flops 2013265920 | bytes 1 | tf_op jit(solution)/shard_map/near/pallas_call | solution.py:106
  36.1 0.9 %collective-permute-done.4 = f32[112,256]{1,0:T(8,128)S(1)} collective-permute-done((f32[112,256]{1,0:T(8,128)S(1)}, f32[112,256]{1,0:T(8,128)S(1)}, u32[]{:S(2)}, u32[]{:S(2)}) %collective-permute-start.4) | collective-permute-done | bytes 114720 | tf_op jit(solution)/shard_map/ppermute | solution.py:200
  37.0 1.4 %collective-permute-done.7 = f32[144,256]{1,0:T(8,128)S(1)} collective-permute-done((f32[144,256]{1,0:T(8,128)S(1)}, f32[144,256]{1,0:T(8,128)S(1)}, u32[]{:S(2)}, u32[]{:S(2)}) %collective-permute-start.7) | collective-permute-done | bytes 147488 | tf_op jit(solution)/shard_map/ppermute | solution.py:198
  38.4 0.0 collective-permute-done.refs_2_
  38.4 0.2 fusion
  38.6 0.1 collective-permute-start.8
  38.7 0.5 collective-permute-start.9
  39.2 0.7 %collective-permute-start.12 = (f32[112,256]{1,0:T(8,128)S(1)}, f32[112,256]{1,0:T(8,128)S(1)}, u32[]{:S(2)}, u32[]{:S(2)}) collective-permute-start(f32[112,256]{1,0:T(8,128)S(1)} %slice.42), channel_id=1, source_target_pairs={{15,16},{16,15},{31,32},{32,31},{47,48},{48,47},{79,80},{80,79},{9... | collective-permute-start | bytes 344072 | tf_op jit(solution)/shard_map/ppermute | solution.py:215
  39.9 0.7 %collective-permute-start.11 = (f32[256,256]{1,0:T(8,128)S(1)}, f32[256,256]{1,0:T(8,128)S(1)}, u32[]{:S(2)}, u32[]{:S(2)}) collective-permute-start(f32[256,256]{1,0:T(8,128)S(1)} %slice.41), channel_id=1, source_target_pairs={{1,2},{2,1},{3,4},{4,3},{5,6},{6,5},{7,8},{8,7},{9,10},{10,9},{11,... | collective-permute-start | bytes 786440 | tf_op jit(solution)/shard_map/ppermute | solution.py:214
  40.6 1.1 %collective-permute-done.8 = f32[256,1280]{1,0:T(8,128)S(1)} collective-permute-done((f32[256,1280]{1,0:T(8,128)S(1)}, f32[256,1280]{1,0:T(8,128)S(1)}, u32[]{:S(2)}, u32[]{:S(2)}) %collective-permute-start.8) | collective-permute-done | bytes 1310752 | tf_op jit(solution)/shard_map/ppermute | solution.py:24
  41.7 8.9 %collective-permute-start.10 = (f32[256,256]{1,0:T(8,128)S(1)}, f32[256,256]{1,0:T(8,128)S(1)}, u32[]{:S(2)}, u32[]{:S(2)}) collective-permute-start(f32[256,256]{1,0:T(8,128)S(1)} %slice.40), channel_id=1, source_target_pairs={{1,2},{2,1},{3,4},{4,3},{5,6},{6,5},{7,8},{8,7},{9,10},{10,9},{11,... | collective-permute-start | bytes 786440 | tf_op jit(solution)/shard_map/ppermute | solution.py:24
  50.6 0.0 collective-permute-done.9
  50.6 0.2 pad_maximum_fusion.refs_5_
  50.8 6.2 %middle.1.refs_2_ = f32[512,1280]{1,0:T(8,128)S(1)} custom-call(bf16[5,512,512]{2,1,0:T(8,128)(2,1)S(1)} %get-tuple-element.12.refs_0_.refs_3_.refs_6_, bf16[5,512,512]{2,1,0:T(8,128)(2,1)S(1)} %get-tuple-element.13.refs_1_.refs_4_.refs_7_, f32[512,1280]{1,0:T(8,128)S(1)} %collective-permute-done.refs_2_, ...), custom_call_target="tpu_custom_call" | custom-call | flops 1 | bytes 1 | tf_op jit(solution)/shard_map/middle/pallas_call | solution.py:106
  57.0 3.3 %collective-permute-done.13.refs_3_ = f32[512,1024]{1,0:T(8,128)S(1)} collective-permute-done((f32[512,1024]{1,0:T(8,128)S(1)}, f32[512,1024]{1,0:T(8,128)S(1)}, u32[]{:S(2)}, u32[]{:S(2)}) %collective-permute-start.13) | collective-permute-done | bytes 2097184 | tf_op jit(solution)/shard_map/ppermute | solution.py:24
  60.2 2.5 %last0.1.refs_6_ = f32[512,1280]{1,0:T(8,128)} custom-call(bf16[5,512,512]{2,1,0:T(8,128)(2,1)S(1)} %get-tuple-element.12.refs_0_.refs_3_.refs_6_, bf16[5,512,512]{2,1,0:T(8,128)(2,1)S(1)} %get-tuple-element.13.refs_1_.refs_4_.refs_7_, f32[512,1280]{1,0:T(8,128)S(1)} %middle.1.refs_2_, f32[512,1024]{1,0:T(8,128)S(1)} %collective-permute-done.13.refs_3_), custom_call_target="tpu_custom_call" | custom-call | flops 1 | bytes 1 | tf_op jit(solution)/shard_map/last0/pallas_call | solution.py:165
  62.8 0.0 collective-permute-done.12.refs_5_
  62.8 0.0 collective-permute-done.11.refs_4_
  62.8 0.3 collective-permute-done.10.refs_3_
  63.0 1.2 %last1.1 = f32[512,1280]{1,0:T(8,128)} custom-call(bf16[5,512,512]{2,1,0:T(8,128)(2,1)S(1)} %get-tuple-element.12.refs_0_.refs_3_.refs_6_, bf16[5,512,512]{2,1,0:T(8,128)(2,1)S(1)} %get-tuple-element.13.refs_1_.refs_4_.refs_7_, f32[512,1280]{1,0:T(8,128)S(1)} %middle.1.refs_2_, ...), custom_call_target="tpu_custom_call", output_to_operand_aliasing={{}: (6, {})} | custom-call | flops 1 | bytes 1 | tf_op jit(solution)/shard_map/last1/pallas_call | solution.py:165
  (6 shorter events, 0.1 us)
Async XLA Ops:
  0.0 38.4 %collective-permute-start = (f32[512,1280]{1,0:T(8,128)}, f32[512,1280]{1,0:T(8,128)S(1)}, u32[]{:S(2)}, u32[]{:S(2)}) collective-permute-start(f32[512,1280]{1,0:T(8,128)} %refs_2_.1), channel_id=1, source_target_pairs={{1,2},{2,1},{3,4},{4,3},{5,6},{6,5},{7,8},{8,7},{9,10},{10,9},{11,... | collective-permute-start | bytes 7864328 | tf_op jit(solution)/shard_map/ppermute | solution.py:24
  8.2 16.9 %copy-start.1 = (f32[512,2176]{1,0:T(8,128)S(1)}, f32[512,2176]{1,0:T(8,128)}, u32[]{:S(2)}) copy-start(f32[512,2176]{1,0:T(8,128)} %v_ref.1) | copy-start | bytes 13369348
  10.2 3.1 %collective-permute-start.1 = (f32[256,1280]{1,0:T(8,128)S(1)}, f32[256,1280]{1,0:T(8,128)S(1)}, u32[]{:S(2)}, u32[]{:S(2)}) collective-permute-start(f32[256,1280]{1,0:T(8,128)S(1)} %get-tuple-element.22), channel_id=1, source_target_pairs={{0,1},{1,0},{2,3},{3,2},{4,5},{5,4},{6,7},{7,6},{8,9},{9,8},{10,11... | collective-permute-start | bytes 3932168 | tf_op jit(solution)/shard_map/ppermute | solution.py:24
  10.3 14.1 %copy-start = (f32[512,1280]{1,0:T(8,128)S(1)}, f32[512,1280]{1,0:T(8,128)}, u32[]{:S(2)}) copy-start(f32[512,1280]{1,0:T(8,128)} %refs_2_.1) | copy-start | bytes 7864324
  10.4 14.8 %copy-start.3 = (s32[4,17]{1,0:T(4,128)S(1)}, s32[4,17]{1,0:T(4,128)}, u32[]{:S(2)}) copy-start(s32[4,17]{1,0:T(4,128)} %pattern_ref.1) | copy-start | bytes 820
  10.4 4.9 %collective-permute-start.2 = (f32[256,1280]{1,0:T(8,128)S(1)}, f32[256,1280]{1,0:T(8,128)S(1)}, u32[]{:S(2)}, u32[]{:S(2)}) collective-permute-start(f32[256,1280]{1,0:T(8,128)S(1)} %get-tuple-element.21), channel_id=1, source_target_pairs={{0,1},{1,0},{2,3},{3,2},{4,5},{5,4},{6,7},{7,6},{8,9},{9,8},{10,11... | collective-permute-start | bytes 3932168 | tf_op jit(solution)/shard_map/ppermute | solution.py:24
  15.4 8.4 %collective-permute-start.5 = (f32[144,256]{1,0:T(8,128)S(1)}, f32[144,256]{1,0:T(8,128)S(1)}, u32[]{:S(2)}, u32[]{:S(2)}) collective-permute-start(f32[144,256]{1,0:T(8,128)S(1)} %slice.33), channel_id=1, source_target_pairs={{255,9},{0,246},{15,25},{16,6},{31,41},{32,22},{47,57},{48,38},{63... | collective-permute-start | bytes 442376 | tf_op jit(solution)/shard_map/ppermute | solution.py:198
  23.8 5.4 %collective-permute-start.6 = (f32[144,256]{1,0:T(8,128)S(1)}, f32[144,256]{1,0:T(8,128)S(1)}, u32[]{:S(2)}, u32[]{:S(2)}) collective-permute-start(f32[144,256]{1,0:T(8,128)S(1)} %collective-permute-done.5), channel_id=1, source_target_pairs={{9,3},{246,252},{25,19},{6,12},{41,35},{22,28},{57,51},{38,44},{73... | collective-permute-start | bytes 442376 | tf_op jit(solution)/shard_map/ppermute | solution.py:198
  24.4 3.2 %collective-permute-start.3 = (f32[112,256]{1,0:T(8,128)S(1)}, f32[112,256]{1,0:T(8,128)S(1)}, u32[]{:S(2)}, u32[]{:S(2)}) collective-permute-start(f32[112,256]{1,0:T(8,128)S(1)} %slice.32), channel_id=1, source_target_pairs={{254,14},{1,241},{62,78},{65,49},{126,142},{129,113},{190,206},{19... | collective-permute-start | bytes 344072 | tf_op jit(solution)/shard_map/ppermute | solution.py:200
  27.2 3.2 %copy-start.2 = (f32[512,1280]{1,0:T(8,128)S(1)}, f32[512,1280]{1,0:T(8,128)}, u32[]{:S(2)}) copy-start(f32[512,1280]{1,0:T(8,128)} %refs_6_.1) | copy-start | bytes 7864324
  27.6 32.7 %collective-permute-start.13 = (f32[512,1024]{1,0:T(8,128)S(1)}, f32[512,1024]{1,0:T(8,128)S(1)}, u32[]{:S(2)}, u32[]{:S(2)}) collective-permute-start(f32[512,1024]{1,0:T(8,128)S(1)} %slice.43), channel_id=1, source_target_pairs={{1,2},{2,1},{3,4},{4,3},{5,6},{6,5},{7,8},{8,7},{9,10},{10,9},{11,... | collective-permute-start | bytes 6291464 | tf_op jit(solution)/shard_map/ppermute | solution.py:24
  27.7 9.3 %collective-permute-start.4 = (f32[112,256]{1,0:T(8,128)S(1)}, f32[112,256]{1,0:T(8,128)S(1)}, u32[]{:S(2)}, u32[]{:S(2)}) collective-permute-start(f32[112,256]{1,0:T(8,128)S(1)} %collective-permute-done.3), channel_id=1, source_target_pairs={{14,0},{241,255},{78,64},{49,63},{142,128},{113,127},{206,192},{17... | collective-permute-start | bytes 344072 | tf_op jit(solution)/shard_map/ppermute | solution.py:200
  29.1 9.2 %collective-permute-start.7 = (f32[144,256]{1,0:T(8,128)S(1)}, f32[144,256]{1,0:T(8,128)S(1)}, u32[]{:S(2)}, u32[]{:S(2)}) collective-permute-start(f32[144,256]{1,0:T(8,128)S(1)} %collective-permute-done.6), channel_id=1, source_target_pairs={{3,0},{252,255},{19,16},{12,15},{35,32},{28,31},{51,48},{44,47},{6... | collective-permute-start | bytes 442376 | tf_op jit(solution)/shard_map/ppermute | solution.py:198
  38.6 3.1 %collective-permute-start.8 = (f32[256,1280]{1,0:T(8,128)S(1)}, f32[256,1280]{1,0:T(8,128)S(1)}, u32[]{:S(2)}, u32[]{:S(2)}) collective-permute-start(f32[256,1280]{1,0:T(8,128)S(1)} %get-tuple-element.19), channel_id=1, source_target_pairs={{0,1},{1,0},{2,3},{3,2},{4,5},{5,4},{6,7},{7,6},{8,9},{9,8},{10,11... | collective-permute-start | bytes 3932168 | tf_op jit(solution)/shard_map/ppermute | solution.py:24
  38.7 11.9 %collective-permute-start.9 = (f32[256,1280]{1,0:T(8,128)S(1)}, f32[256,1280]{1,0:T(8,128)S(1)}, u32[]{:S(2)}, u32[]{:S(2)}) collective-permute-start(f32[256,1280]{1,0:T(8,128)S(1)} %get-tuple-element.20), channel_id=1, source_target_pairs={{0,1},{1,0},{2,3},{3,2},{4,5},{5,4},{6,7},{7,6},{8,9},{9,8},{10,11... | collective-permute-start | bytes 3932168 | tf_op jit(solution)/shard_map/ppermute | solution.py:24
  39.2 23.6 %collective-permute-start.12 = (f32[112,256]{1,0:T(8,128)S(1)}, f32[112,256]{1,0:T(8,128)S(1)}, u32[]{:S(2)}, u32[]{:S(2)}) collective-permute-start(f32[112,256]{1,0:T(8,128)S(1)} %slice.42), channel_id=1, source_target_pairs={{15,16},{16,15},{31,32},{32,31},{47,48},{48,47},{79,80},{80,79},{9... | collective-permute-start | bytes 344072 | tf_op jit(solution)/shard_map/ppermute | solution.py:215
  39.9 22.9 %collective-permute-start.11 = (f32[256,256]{1,0:T(8,128)S(1)}, f32[256,256]{1,0:T(8,128)S(1)}, u32[]{:S(2)}, u32[]{:S(2)}) collective-permute-start(f32[256,256]{1,0:T(8,128)S(1)} %slice.41), channel_id=1, source_target_pairs={{1,2},{2,1},{3,4},{4,3},{5,6},{6,5},{7,8},{8,7},{9,10},{10,9},{11,... | collective-permute-start | bytes 786440 | tf_op jit(solution)/shard_map/ppermute | solution.py:214
  41.7 21.3 %collective-permute-start.10 = (f32[256,256]{1,0:T(8,128)S(1)}, f32[256,256]{1,0:T(8,128)S(1)}, u32[]{:S(2)}, u32[]{:S(2)}) collective-permute-start(f32[256,256]{1,0:T(8,128)S(1)} %slice.40), channel_id=1, source_target_pairs={{1,2},{2,1},{3,4},{4,3},{5,6},{6,5},{7,8},{8,7},{9,10},{10,9},{11,... | collective-permute-start | bytes 786440 | tf_op jit(solution)/shard_map/ppermute | solution.py:24
